TPU v7x, 256 devices: a whole 4x4x8 slice. The times are simulated.
256 devices in a mesh: dp: 2 (over core), ctx: 8 (over z), resp: 16 (over x, y).
Axes of the slice: x: 4, y: 4, z: 8, core: 2. Of those that a mesh axis runs over, the one named last changes fastest.
Arguments:
- prompt_x: bfloat16 [2, 32768, 4096], P('dp', ('ctx', 'resp')), may hold values from -6 to 6
- prompt_b: bfloat16 [2, 32768, 128], P('dp', ('ctx', 'resp')), may hold values from -0.75 to 0.75
- prompt_dt: float32 [2, 32768, 64], P('dp', ('ctx', 'resp')), may hold values from -6 to 7
- prompt_states: bfloat16 [2, 128, 64, 64, 128], P('dp', ('ctx', 'resp')), may hold values from -6 to 6
- resp_x: bfloat16 [2, 16, 2048, 4096], P('dp', 'resp', 'ctx'), may hold values from -6 to 6
- resp_b: bfloat16 [2, 16, 2048, 128], P('dp', 'resp', 'ctx'), may hold values from -0.75 to 0.75
- resp_c: bfloat16 [2, 16, 2048, 128], P('dp', 'resp', 'ctx'), may hold values from -0.75 to 0.75
- resp_dt: float32 [2, 16, 2048, 64], P('dp', 'resp', 'ctx'), may hold values from -6 to 7
- grad_out: bfloat16 [2, 16, 2048, 4096], P('dp', 'resp', 'ctx'), may hold values from -0.625 to 0.625
- lengths: int32 [2, 16], P('dp', 'resp'), may hold values from 256 to 2048, as said below
- advantages: float32 [2, 16], P('dp', 'resp'), may hold values from -6 to 6
- dt_bias: float32 [64], replicated, may hold values from -1 to 0.5
- a_log: float32 [64], replicated, may hold values from -20 to -2
- skip: float32 [64], replicated, may hold values from 0.5 to 1.5
Outputs:
- prompt_dx: bfloat16 [2, 32768, 4096], P('dp', ('ctx', 'resp'))
- prompt_db: float32 [2, 32768, 128], P('dp', ('ctx', 'resp'))
- prompt_ddt: float32 [2, 32768, 64], P('dp', ('ctx', 'resp'))
- resp_dx: bfloat16 [2, 16, 2048, 4096], P('dp', 'resp', 'ctx')
- resp_db: float32 [2, 16, 2048, 128], P('dp', 'resp', 'ctx')
- resp_dc: float32 [2, 16, 2048, 128], P('dp', 'resp', 'ctx')
- resp_ddt: float32 [2, 16, 2048, 64], P('dp', 'resp', 'ctx')
- grad_bias: float32 [64], replicated
- grad_alog: float32 [64], replicated
- grad_skip: float32 [64], replicated
Inputs may be any that keep to these rules, and one draw needn't show every extreme that they name: `lengths`: at least 256; in every group one response has exactly 2048 tokens.
All inputs are finite; a program needn't handle non-finite values.
Results may differ from a plain program's by a relative error of at most 0.0011.
Values sent between devices are 32-bit elements; how exact they have to be, the bound alone decides.
A program may use at most 192 MiB of HBM per device.

v0:
```python
import math

import jax
import jax.numpy as jnp
from jax import lax
from jax.sharding import PartitionSpec as P

precise = lax.Precision.HIGHEST


def spread_2(shard, axis, root):
    mine = lax.axis_index(axis) == root
    return lax.psum(jnp.where(mine, shard, jnp.zeros_like(shard)), axis)


def carried_in(shard, axis, combine, identity, reverse):
    devices, here = (lax.axis_size(axis), lax.axis_index(axis))
    everything = jax.tree.map(lambda part: lax.all_gather(part, axis), shard)
    start = jax.tree.map(
        lambda part, zero: jnp.broadcast_to(jnp.asarray(zero, part.dtype), part.shape),
        shard,
        identity,
    )

    def turn(k, before):
        at = devices - 1 - k if reverse else k
        reached = at > here if reverse else at < here
        new = combine(before, jax.tree.map(lambda part: part[at], everything))
        return jax.tree.map(lambda a, b: jnp.where(reached, a, b), new, before)

    return lax.fori_loop(0, devices, turn, start)


def decay_terms(raw_step, step_bias, log_rate):
    step_size = jax.nn.softplus(raw_step + step_bias)
    running = jnp.cumsum(-jnp.exp(log_rate) * step_size, axis=0)
    return (step_size, running)


def block_output(inputs, b_proj, c_proj, raw_step, step_bias, log_rate, skip_gain, state_in):
    step_size, running = decay_terms(raw_step, step_bias, log_rate)
    tokens_in = inputs.shape[0]
    causal = jnp.arange(tokens_in)[:, None] >= jnp.arange(tokens_in)[None, :]
    spread = running.T[:, :, None] - running.T[:, None, :]
    kernel = jnp.exp(jnp.where(causal[None], spread, -jnp.inf))
    scores = jnp.dot(c_proj, b_proj.T, precision=precise)
    weights = kernel * scores[None] * step_size.T[:, None, :]
    within = jnp.einsum("hts,shp->thp", weights, inputs, precision=precise)
    carried = jnp.exp(running)[:, :, None] * jnp.einsum(
        "tn,hpn->thp", c_proj, state_in, precision=precise
    )
    return within + carried + skip_gain[None, :, None] * inputs


def block_state(inputs, b_proj, raw_step, step_bias, log_rate, state_in):
    step_size, running = decay_terms(raw_step, step_bias, log_rate)
    closing = running[-1]
    toward = jnp.exp(closing[None, :] - running) * step_size
    driven = toward[:, :, None] * inputs
    return jnp.exp(closing)[:, None, None] * state_in + jnp.einsum(
        "shp,sn->hpn", driven, b_proj, precision=precise
    )


def response_block(
    inputs,
    b_proj,
    c_proj,
    raw_step,
    step_bias,
    log_rate,
    skip_gain,
    state_in,
    cotangent,
    state_grad,
):

    def response_forward(
        inputs, b_proj, c_proj, raw_step, step_bias, log_rate, skip_gain, state_in
    ):
        return (
            block_output(
                inputs, b_proj, c_proj, raw_step, step_bias, log_rate, skip_gain, state_in
            ),
            block_state(inputs, b_proj, raw_step, step_bias, log_rate, state_in),
        )

    unused, pullback = jax.vjp(
        response_forward, inputs, b_proj, c_proj, raw_step, step_bias, log_rate, skip_gain, state_in
    )
    return pullback((cotangent, state_grad))


def prompt_block(inputs, b_proj, raw_step, step_bias, log_rate, state_in, state_grad):

    def prompt_forward(inputs, b_proj, raw_step, step_bias, log_rate):
        return block_state(inputs, b_proj, raw_step, step_bias, log_rate, state_in)

    unused, pullback = jax.vjp(prompt_forward, inputs, b_proj, raw_step, step_bias, log_rate)
    return pullback(state_grad)


def by_heads(values, blocks):
    old_shape = values.shape
    reshaped = values.reshape((old_shape[0], blocks, old_shape[1] // blocks) + old_shape[2:])
    return jnp.moveaxis(reshaped, 1, 0)


def from_heads(values):
    shifted = jnp.moveaxis(values, 0, 1)
    return shifted.reshape(
        (shifted.shape[0], shifted.shape[1] * shifted.shape[2]) + shifted.shape[3:]
    )


def head_first(values, blocks):
    return values.reshape((blocks, values.shape[0] // blocks) + values.shape[1:])


def head_back(values):
    return values.reshape((values.shape[0] * values.shape[1],) + values.shape[2:])


def response_grads(
    inputs,
    b_proj,
    c_proj,
    raw_step,
    step_bias,
    log_rate,
    skip_gain,
    state_in,
    cotangent,
    state_grad,
):
    head_count = inputs.shape[1]
    blocks = head_count // math.gcd(head_count, 16)

    def response_per_block(pieces):
        return response_block(
            pieces[0],
            b_proj,
            c_proj,
            pieces[1],
            pieces[2],
            pieces[3],
            pieces[4],
            pieces[5],
            pieces[6],
            pieces[7],
        )

    results = lax.map(
        response_per_block,
        (
            by_heads(inputs, blocks),
            by_heads(raw_step, blocks),
            head_first(step_bias, blocks),
            head_first(log_rate, blocks),
            head_first(skip_gain, blocks),
            head_first(state_in, blocks),
            by_heads(cotangent, blocks),
            head_first(state_grad, blocks),
        ),
    )
    return (
        from_heads(results[0]),
        jnp.sum(results[1], axis=0),
        jnp.sum(results[2], axis=0),
        from_heads(results[3]),
        head_back(results[4]),
        head_back(results[5]),
        head_back(results[6]),
        head_back(results[7]),
    )


def prompt_grads(inputs, b_proj, raw_step, step_bias, log_rate, state_in, state_grad):
    head_count = inputs.shape[1]
    blocks = head_count // math.gcd(head_count, 16)

    def prompt_per_block(pieces):
        return prompt_block(
            pieces[0], b_proj, pieces[1], pieces[2], pieces[3], pieces[4], pieces[5]
        )

    results = lax.map(
        prompt_per_block,
        (
            by_heads(inputs, blocks),
            by_heads(raw_step, blocks),
            head_first(step_bias, blocks),
            head_first(log_rate, blocks),
            head_first(state_in, blocks),
            head_first(state_grad, blocks),
        ),
    )
    return (
        from_heads(results[0]),
        jnp.sum(results[1], axis=0),
        from_heads(results[2]),
        head_back(results[3]),
        head_back(results[4]),
    )


def join(earlier, later):
    return (earlier[0] * later[0], later[0][:, None, None] * earlier[1] + later[1])


def multiply(earlier, later):
    return earlier * later


def body(
    prompt_x,
    prompt_b,
    prompt_dt,
    prompt_states,
    resp_x,
    resp_b,
    resp_c,
    resp_dt,
    grad_out,
    lengths,
    advantages,
    dt_bias,
    a_log,
    skip,
):
    head_count = dt_bias.shape[0]
    model_width = prompt_x.shape[2]
    head_dim = model_width // head_count
    state_dim = prompt_b.shape[2]
    prompt_blocks = prompt_states.shape[1]
    block_len = prompt_x.shape[1] // prompt_blocks
    answer_blocks = resp_x.shape[2] // block_len
    answer_rows = answer_blocks * block_len
    state_shape = (head_count, head_dim, state_dim)
    no_state = jnp.zeros(state_shape, jnp.float32)
    no_decay = jnp.ones((head_count,), jnp.float32)
    plain_x = (
        prompt_x[0].astype(jnp.float32).reshape(prompt_blocks, block_len, head_count, head_dim)
    )
    plain_b = prompt_b[0].astype(jnp.float32).reshape(prompt_blocks, block_len, state_dim)
    plain_dt = prompt_dt[0].reshape(prompt_blocks, block_len, head_count)
    saved = prompt_states[0].astype(jnp.float32)
    last_state = block_state(
        plain_x[prompt_blocks - 1],
        plain_b[prompt_blocks - 1],
        plain_dt[prompt_blocks - 1],
        dt_bias,
        a_log,
        saved[prompt_blocks - 1],
    )
    end_state = spread_2(last_state, ("ctx", "resp"), lax.axis_size(("ctx", "resp")) - 1)
    ans_x = resp_x[0, 0].astype(jnp.float32).reshape(answer_blocks, block_len, head_count, head_dim)
    ans_b = resp_b[0, 0].astype(jnp.float32).reshape(answer_blocks, block_len, state_dim)
    ans_c = resp_c[0, 0].astype(jnp.float32).reshape(answer_blocks, block_len, state_dim)
    ans_dt = resp_dt[0, 0].reshape(answer_blocks, block_len, head_count)
    local_decay, local_fresh, local_running = ([], [], [])
    forward_total = (no_decay, no_state)
    block_idx = 0
    running = decay_terms(ans_dt[block_idx], dt_bias, a_log)[1]
    decay_now = jnp.exp(running[-1])
    fresh_state = block_state(
        ans_x[block_idx], ans_b[block_idx], ans_dt[block_idx], dt_bias, a_log, no_state
    )
    local_decay.append(decay_now)
    local_fresh.append(fresh_state)
    local_running.append(running)
    forward_total = join(forward_total, (decay_now, fresh_state))
    prefix = carried_in(forward_total, "ctx", join, (no_decay, no_state), False)
    state_now = prefix[0][:, None, None] * end_state + prefix[1]
    block_idx = 0
    starts = [state_now]
    position = lax.axis_index("ctx") * answer_rows + jnp.arange(answer_rows)
    length_now = lengths[0, 0]
    factor = (
        advantages[0, 0] * (answer_rows * lax.axis_size("ctx")) / length_now.astype(jnp.float32)
    )
    cotangent = (
        grad_out[0, 0].astype(jnp.float32) * jnp.where(position < length_now, factor, 0.0)[:, None]
    )
    cotangent = cotangent.reshape(answer_blocks, block_len, head_count, head_dim)
    backward_total = (no_decay, no_state)
    for block_idx in reversed(range(answer_blocks)):
        weighted = jnp.exp(local_running[block_idx])[:, :, None] * cotangent[block_idx]
        entry_grad = jnp.einsum("tn,thp->hpn", ans_c[block_idx], weighted, precision=precise)
        backward_total = join(backward_total, (local_decay[block_idx], entry_grad))
    suffix = carried_in(backward_total, "ctx", join, (no_decay, no_state), True)
    state_grad = suffix[1]
    resp_parts = []
    for block_idx in reversed(range(answer_blocks)):
        results = response_grads(
            ans_x[block_idx],
            ans_b[block_idx],
            ans_c[block_idx],
            ans_dt[block_idx],
            dt_bias,
            a_log,
            skip,
            starts[block_idx],
            cotangent[block_idx],
            state_grad,
        )
        state_grad = results[7]
        resp_parts.insert(0, results)
    on_first = lax.axis_index("ctx") == 0
    start_grad = jnp.where(on_first, state_grad, 0.0)
    seed_grad = lax.psum(start_grad, ("ctx", "resp"))
    device_decay = no_decay
    block_idx = 0
    decay_now = jnp.exp(decay_terms(plain_dt[block_idx], dt_bias, a_log)[1][-1])
    prompt_decay = [decay_now]
    device_decay = device_decay * decay_now
    follow = carried_in(device_decay, ("ctx", "resp"), multiply, no_decay, True)
    prompt_parts = []
    for block_idx in reversed(range(prompt_blocks)):
        results = prompt_grads(
            plain_x[block_idx],
            plain_b[block_idx],
            plain_dt[block_idx],
            dt_bias,
            a_log,
            saved[block_idx],
            follow[:, None, None] * seed_grad,
        )
        follow = follow * prompt_decay[block_idx]
        prompt_parts.insert(0, results)
    prompt_dx = jnp.concatenate(
        [parts[0].reshape(block_len, model_width) for parts in prompt_parts], axis=0
    )
    prompt_db = jnp.concatenate([parts[1] for parts in prompt_parts], axis=0)
    prompt_ddt = jnp.concatenate([parts[2] for parts in prompt_parts], axis=0)
    resp_dx = jnp.concatenate(
        [parts[0].reshape(block_len, model_width) for parts in resp_parts], axis=0
    )
    resp_db = jnp.concatenate([parts[1] for parts in resp_parts], axis=0)
    resp_dc = jnp.concatenate([parts[2] for parts in resp_parts], axis=0)
    resp_ddt = jnp.concatenate([parts[3] for parts in resp_parts], axis=0)
    local_bias = sum([parts[3] for parts in prompt_parts]) + sum([parts[4] for parts in resp_parts])
    local_alog = sum([parts[4] for parts in prompt_parts]) + sum([parts[5] for parts in resp_parts])
    local_skip = sum([parts[6] for parts in resp_parts])
    grad_bias, grad_alog, grad_skip = lax.psum(
        (local_bias, local_alog, local_skip), ("dp", "ctx", "resp")
    )
    return (
        prompt_dx.astype(jnp.bfloat16)[None],
        prompt_db[None],
        prompt_ddt[None],
        resp_dx.astype(jnp.bfloat16)[None, None],
        resp_db[None, None],
        resp_dc[None, None],
        resp_ddt[None, None],
        grad_bias,
        grad_alog,
        grad_skip,
    )


def solution(mesh):
    in_specs = (
        P("dp", ("ctx", "resp"), None),
        P("dp", ("ctx", "resp"), None),
        P("dp", ("ctx", "resp"), None),
        P("dp", ("ctx", "resp"), None, None, None),
        P("dp", "resp", "ctx", None),
        P("dp", "resp", "ctx", None),
        P("dp", "resp", "ctx", None),
        P("dp", "resp", "ctx", None),
        P("dp", "resp", "ctx", None),
        P("dp", "resp"),
        P("dp", "resp"),
        P(),
        P(),
        P(),
    )
    out_specs = (
        P("dp", ("ctx", "resp"), None),
        P("dp", ("ctx", "resp"), None),
        P("dp", ("ctx", "resp"), None),
        P("dp", "resp", "ctx", None),
        P("dp", "resp", "ctx", None),
        P("dp", "resp", "ctx", None),
        P("dp", "resp", "ctx", None),
        P(),
        P(),
        P(),
    )
    return jax.shard_map(body, mesh=mesh, in_specs=in_specs, out_specs=out_specs, check_vma=False)
```

profile of v0, /device:TPU:1, one launch (start us, length us, event | category | flops | bytes accessed | tf_op | source)
XLA Modules:
  0.0 1200.6 jit_solution(962990033951420877)
XLA Ops:
  38.3 5.8 fusion.114
  44.1 4.0 transpose.174
  50.9 17.4 %all-gather.3 = f32[8,1,64]{2,1,0:T(1,128)S(1)} all-gather(f32[1,1,64]{2,1,0:T(1,128)S(1)} %bitcast.744), channel_id=1, replica_groups=mesh['dp'=2,'ctx'=8,'resp'=16] {'ctx'}, dimensions={0}, use_global_device_ids=true | all-gather | bytes 2304 | tf_op jit(solution)/shard_map/all_gather | solution.py:18
  68.3 4.2 multiply_bitcast_fusion
  72.5 295.1 %all-gather.2 = f32[128,1,64]{2,1,0:T(1,128)} all-gather(f32[1,1,64]{2,1,0:T(1,128)S(1)} %bitcast.743), channel_id=1, replica_groups=mesh['dp'=2,'ctx'=8,'resp'=16] {'ctx','resp'}, dimensions={0}, use_global_device_ids=true | all-gather | bytes 33024 | tf_op jit(solution)/shard_map/all_gather | solution.py:18
  367.7 30.5 %while.100 = (s32[]{:T(128)}, f32[64]{0:T(128)S(1)}, f32[64,64,128]{2,1,0:T(8,128)}, s32[]{:T(128)}, f32[8,64]{1,0:T(8,128)S(1)}, /*index=5*/f32[8,64,64,128]{3,2,1,0:T(8,128)}) while((s32[]{:T(128)}, f32[64]{0:T(128)S(1)}, f32[64,64,128]{2,1,0:T(8,128)}, s32[]{:T(128)}, f32[8,64]{1,0:T(8,128)S(1)}, ...), condition=%wide.region_7.8_spmd.clone.clone, body=%wide.region_6.7_spmd.clone.sunk.clone | while | flops 2097348 | bytes 6292835 | solution.py:31
  370.9 3.9 fusion.245
  374.8 3.9 fusion.245
  378.7 3.9 fusion.245
  382.6 3.9 fusion.245
  390.4 3.9 fusion.245
  394.3 3.9 fusion.245
  398.2 17.1 %while.99 = (s32[]{:T(128)}, f32[64,64,128]{2,1,0:T(8,128)S(1)}, s32[]{:T(128)}, f32[8,64]{1,0:T(8,128)S(1)}, f32[8,64,64,128]{3,2,1,0:T(8,128)}) while((s32[]{:T(128)}, f32[64,64,128]{2,1,0:T(8,128)S(1)}, s32[]{:T(128)}, f32[8,64]{1,0:T(8,128)S(1)}, f32[8,64,64,128]{3,2,1,0:T(8,128)}) %tuple.264), condition=%wide.region_10.11_spmd.clone.clone, body=%wide.region_9.10_spmd.clone.sunk.clone | while | flops 2097160 | bytes 6292359 | solution.py:31
  415.3 111.2 %all-reduce.6.cloned.1.call-done = f32[64,64,128]{2,1,0:T(8,128)} async-done(((f32[64,64,128]{2,1,0:T(8,128)}), f32[64,64,128]{2,1,0:T(8,128)}) %all-reduce.6.cloned.1.call-update) | async-done | bytes 2097168 | tf_op jit(solution)/shard_map/psum | solution.py:13
  536.1 223.2 %while.96 = (s32[]{:T(128)}, bf16[4,256,16,64]{1,3,2,0:T(8,128)(2,1)}, f32[4,256,128]{2,1,0:T(8,128)}, f32[4,256,128]{2,1,0:T(8,128)}, f32[4,256,16]{2,1,0:T(8,1...) while((s32[]{:T(128)}, ...), condition=%wide.region_31.33_spmd.clone, body=%wide.region_11.32_spmd.sunk.clone | while | flops 3848802304 | bytes 44009176 | solution.py:153
  551.2 4.1 fusion.225
  555.6 8.5 fusion.228
  593.6 5.6 fusion.231
  604.2 4.1 fusion.225
  608.6 8.5 fusion.228
  646.6 5.6 fusion.231
  657.1 4.1 fusion.225
  661.6 8.5 fusion.228
  699.6 5.6 fusion.231
  710.1 4.1 fusion.225
  714.5 8.5 fusion.228
  752.5 5.6 fusion.231
  763.2 88.3 %while.98 = (s32[]{:T(128)}, f32[64]{0:T(128)S(1)}, s32[]{:T(128)}, f32[128,64]{1,0:T(8,128)}) while((s32[]{:T(128)}, f32[64]{0:T(128)S(1)}, s32[]{:T(128)}, f32[128,64]{1,0:T(8,128)}) %tuple.262), condition=%wide.region_3.4_spmd.clone.clone, body=%wide.region_2.3_spmd.clone.sunk.clone | while | flops 200 | bytes 891 | solution.py:31
  862.3 122.6 %all-reduce.8.cloned.1.call-done = f32[64,64,128]{2,1,0:T(8,128)} async-done(((f32[64,64,128]{2,1,0:T(8,128)}), f32[64,64,128]{2,1,0:T(8,128)}) %all-reduce.8.cloned.1.call-update) | async-done | bytes 2097168 | tf_op jit(solution)/shard_map/psum | solution.py:311
  991.2 115.4 %while.97 = (s32[]{:T(128)}, bf16[4,256,16,64]{1,3,2,0:T(8,128)(2,1)}, f32[4,256,128]{2,1,0:T(8,128)}, f32[4,256,16]{2,1,0:T(8,128)}, f32[4,16]{1,0:T(4,128)}, /...) while((s32[]{:T(128)}, ...), condition=%wide.region_43.45_spmd.clone, body=%wide.region_33.44_spmd.sunk.clone | while | flops 807833728 | bytes 9543665 | solution.py:187
  1108.0 4.2 copy.195
  1113.7 79.1 %all-reduce.2 = (f32[64]{0:T(128)}, f32[64]{0:T(128)}, f32[64]{0:T(128)}) all-reduce(f32[64]{0:T(128)S(1)} %add.237, f32[64]{0:T(128)S(1)} %add.239, f32[64]{0:T(128)S(1)} %copy-done.38), channel_id=1, replica_groups=mesh['dp'=2,'ctx'=8,'resp'=16] {'dp','ctx','resp'}, use_global_device_ids=true, to_apply=%region_47.49 | all-reduce | flops 192 | bytes 1536 | tf_op jit(solution)/shard_map/psum | solution.py:345
  (755 shorter events, 431.1 us)
Async XLA Ops:
  8.0 359.6 %all-gather.9.cloned.1.call-start = ((), (), s32[]{:S(2)}) async-start(), calls=%async_computation.3 | async-start | bytes 18874368 | tf_op jit(solution)/shard_map/all_gather | solution.py:18
  21.8 376.3 %all-gather.7.cloned.1.call-start = ((), (), s32[]{:S(2)}) async-start(), calls=%async_computation.2 | async-start | bytes 18874368 | tf_op jit(solution)/shard_map/all_gather | solution.py:18
  32.0 494.5 %all-reduce.6.cloned.1.call-start = ((), (), s32[]{:S(2)}) async-start(), calls=%async_computation | async-start | bytes 4194304 | tf_op jit(solution)/shard_map/psum | solution.py:13
  44.0 940.8 %all-reduce.8.cloned.1.call-start = ((), (), s32[]{:S(2)}) async-start(), calls=%async_computation.1 | async-start | bytes 4194304 | tf_op jit(solution)/shard_map/psum | solution.py:311
  555.5 8.5 copy-start.23
  555.6 8.5 copy-start.19
  581.4 12.1 %copy-start.1 = (f32[256,16,64]{0,2,1:T(8,128)S(1)}, f32[256,16,64]{0,2,1:T(8,128)}, u32[]{:S(2)}) copy-start(f32[256,16,64]{0,2,1:T(8,128)} %get-tuple-element.1338) | copy-start | bytes 3145732 | tf_op jit(solution)/shard_map/while
  585.1 8.5 copy-start
  585.1 8.5 copy-start.16
  585.1 8.5 copy-start.18
  585.1 8.5 copy-start.20
  585.1 8.5 copy-start.24
  585.1 8.5 copy-start.31
  608.5 8.5 copy-start.23
  608.6 8.5 copy-start.19
  634.4 12.1 %copy-start.1 = (f32[256,16,64]{0,2,1:T(8,128)S(1)}, f32[256,16,64]{0,2,1:T(8,128)}, u32[]{:S(2)}) copy-start(f32[256,16,64]{0,2,1:T(8,128)} %get-tuple-element.1338) | copy-start | bytes 3145732 | tf_op jit(solution)/shard_map/while
  638.1 8.5 copy-start.24
  638.1 8.5 copy-start.31
  661.5 8.5 copy-start.23
  661.5 8.5 copy-start.19
  687.4 12.1 %copy-start.1 = (f32[256,16,64]{0,2,1:T(8,128)S(1)}, f32[256,16,64]{0,2,1:T(8,128)}, u32[]{:S(2)}) copy-start(f32[256,16,64]{0,2,1:T(8,128)} %get-tuple-element.1338) | copy-start | bytes 3145732 | tf_op jit(solution)/shard_map/while
  691.0 8.5 copy-start.18
  691.0 8.5 copy-start.20
  691.1 8.5 copy-start.24
  691.1 8.5 copy-start.31
  714.5 8.5 copy-start.23
  714.5 8.5 copy-start.19
  740.3 12.1 %copy-start.1 = (f32[256,16,64]{0,2,1:T(8,128)S(1)}, f32[256,16,64]{0,2,1:T(8,128)}, u32[]{:S(2)}) copy-start(f32[256,16,64]{0,2,1:T(8,128)} %get-tuple-element.1338) | copy-start | bytes 3145732 | tf_op jit(solution)/shard_map/while
  744.0 8.5 copy-start.20
  744.0 8.5 copy-start.24
  744.1 8.5 copy-start.31
  762.6 89.0 %copy-start.3 = (bf16[1,256,4096]{1,2,0:T(8,128)(2,1)S(1)}, bf16[1,256,4096]{1,2,0:T(8,128)(2,1)}, u32[]{:S(2)}) copy-start(bf16[1,256,4096]{1,2,0:T(8,128)(2,1)} %copy-done.2) | copy-start | bytes 6291460
  (65 other events, 288.9 us)
Sparse Core Ops, SparseCore 0:
  21.9 185.0 all-gather.8
  208.8 172.8 all-gather.6
Sparse Core Ops, SparseCore 1:
  44.1 482.3 all-reduce.5
  762.7 222.1 all-reduce.7
where the time goes:
time: 1220 us; the launch traced here: 1200 us
  blocking collectives  392 us (32%)
  other arithmetic  261 us (21%)
  waiting for transfers between devices  234 us (19%)
  matrix products  174 us (14%)
  local copies, waits for them, and re-layouts  111 us (9%)
  between operations  17.5 us (1%)
  loops' own time  12.7 us (1%)
    all_gather x2, blocking collectives, carried_in(): everything = jax.tree.map(lambda part: lax.all_gather(part, axis), shard)  312 us
    select_n x152, other arithmetic, turn(): return jax.tree.map(lambda a, b: jnp.where(reached, a, b), new, before)  135 us
    psum x1, waiting for transfers between devices, body(): seed_grad = lax.psum(start_grad, ('ctx', 'resp'))  123 us
    psum x1, waiting for transfers between devices, spread_2(): return lax.psum(jnp.where(mine, shard, jnp.zeros_like(shard)), axis)  111 us
    psum x1, blocking collectives, body(): lax.psum((local_bias, local_alog, local_skip), ('dp', 'ctx', 'resp'))  79.1 us
    dot_general x18, matrix products, block_state(): jnp.einsum('shp,sn->hpn', driven, b_proj, precision=precise)  61.6 us
    dot_general x8, matrix products, block_output(): within = jnp.einsum('hts,shp->thp', weights, inputs, precision=precise)  56.2 us
    another operation x70, other arithmetic  48.7 us
  transfers between devices with their start and end apart: 4, of which 2 were waited for; matrix products, arithmetic and copies ran while one was open for 15% of the time, Pallas kernels for 0%

commit v1 on v0

v1 whole, which is shorter than its diff:
```python
import functools

import jax
import jax.numpy as jnp
from jax import lax
from jax.experimental import pallas as pl
from jax.experimental.pallas import tpu as pltpu
from jax.sharding import PartitionSpec as P

MESH = pl.DeviceIdType.MESH
F32 = jnp.float32
BF16 = jnp.bfloat16
TOK = 256
LANES = 256
PER = 4
NH = 64
HD = 64
NS = 128
CHUNKS = 16
PAIRS = 32
LIMIT = 56 * 1024 * 1024


def nn(a, b):
    return lax.dot_general(a, b, (((1,), (0,)), ((), ())), preferred_element_type=F32)


def nt(a, b):
    return lax.dot_general(a, b, (((1,), (1,)), ((), ())), preferred_element_type=F32)


def split2(v):
    hi = v.astype(BF16)
    return hi, (v - hi.astype(F32)).astype(BF16)


def split3(v):
    hi = v.astype(BF16)
    rest = v - hi.astype(F32)
    mid = rest.astype(BF16)
    return hi, mid, (rest - mid.astype(F32)).astype(BF16)


def exact_nn(tri, v):
    hi, mid, lo = split3(v)
    return nn(tri, hi) + (nn(tri, mid) + nn(tri, lo))


def iota(shape, dim):
    return lax.broadcasted_iota(jnp.int32, shape, dim)


def lower():
    return jnp.where(iota((TOK, TOK), 0) >= iota((TOK, TOK), 1), 1.0, 0.0).astype(BF16)


def upper():
    return jnp.where(iota((TOK, TOK), 0) <= iota((TOK, TOK), 1), 1.0, 0.0).astype(BF16)


def spreader(c, rows):
    head = iota((rows, LANES), 0) & (NH - 1)
    lane = iota((rows, LANES), 1) >> 6
    return jnp.where(head == lane + c * PER, 1.0, 0.0).astype(BF16)


def steps(dt, bias, alog):
    z = dt + bias
    d = jnp.maximum(z, 0.0) + jnp.log1p(jnp.exp(-jnp.abs(z)))
    rate = -jnp.exp(alog)
    a = exact_nn(lower(), rate * d)
    return z, d, rate, a


def cat2(v):
    hi, lo = split2(v)
    return jnp.concatenate([hi, lo], axis=1)


def by_head(v, spread):
    hi, lo = split2(v)
    return nt(hi, spread) + nt(lo, spread)


def fold8(v):
    total = v[0:8]
    for at in range(8, v.shape[0], 8):
        total = total + v[at : at + 8]
    return total


def row_mask(length_ref):
    position = lax.axis_index("ctx") * TOK + iota((TOK, 1), 0)
    return jnp.where(position < length_ref[0, 0], 1.0, 0.0)


def first_kernel(
    len_ref, rx_ref, rb_ref, rc_ref, rdt_ref, gy_ref, px_ref, pb_ref, pdt_ref, ps_ref, bias_ref, alog_ref,
    fresh_ref, entry_ref, end_ref,
    wcat, ecat, bt, ct, pwcat, pecat, pbt,
):
    c = pl.program_id(0)
    last = (lax.axis_index("ctx") == lax.axis_size("ctx") - 1) & (
        lax.axis_index("resp") == lax.axis_size("resp") - 1
    )

    @pl.when(c == 0)
    def _():
        bias, alog = bias_ref[...], alog_ref[...]
        _, d, _, a = steps(rdt_ref[...], bias, alog)
        wcat[...] = cat2(jnp.exp(a[TOK - 1 :, :] - a) * d)
        ecat[...] = cat2(jnp.exp(a) * row_mask(len_ref))
        bt[...] = rb_ref[...].astype(F32).T.astype(BF16)
        ct[...] = rc_ref[...].astype(F32).T.astype(BF16)

    @pl.when((c == 0) & last)
    def _():
        bias, alog = bias_ref[...], alog_ref[...]
        _, d, _, a = steps(pdt_ref[...], bias, alog)
        pwcat[...] = cat2(jnp.exp(a[TOK - 1 :, :] - a) * d)
        pecat[...] = cat2(jnp.broadcast_to(jnp.exp(a[TOK - 1 :, :]), (NS, NH)))
        pbt[...] = pb_ref[...].astype(F32).T.astype(BF16)

    spread = spreader(c, 2 * NH)

    def put(ref, value):
        ref[0] = value[:, :128]
        ref[1] = value[:, 128:]

    hi, lo = split2(nn(wcat[...], spread) * rx_ref[...].astype(F32))
    put(fresh_ref, nn(bt[...], hi) + nn(bt[...], lo))
    hi, lo = split2(nn(ecat[...], spread) * gy_ref[...].astype(F32))
    put(entry_ref, nn(ct[...], hi) + nn(ct[...], lo))

    @pl.when(last)
    def _():
        hi, lo = split2(nn(pwcat[...], spread) * px_ref[...].astype(F32))
        eye = jnp.where(iota((NS, NS), 0) == iota((NS, NS), 1), 1.0, 0.0).astype(BF16)
        saved = nt(eye, ps_ref[...])
        put(end_ref, nn(pecat[...], spread) * saved + (nn(pbt[...], hi) + nn(pbt[...], lo)))

    @pl.when(jnp.logical_not(last))
    def _():
        end_ref[...] = jnp.zeros_like(end_ref)


def first_call(length, rx, rb, rc, rdt, gy, px, pb, pdt, ps, bias, alog):
    wide = pl.BlockSpec((TOK, LANES), lambda c: (0, c))
    whole = lambda shape: pl.BlockSpec(shape, lambda c: (0,) * len(shape))
    state = pl.BlockSpec((2, NS, 128), lambda c: (c, 0, 0))
    shape = jax.ShapeDtypeStruct((PAIRS, NS, 128), F32)
    return pl.pallas_call(
        first_kernel,
        grid=(CHUNKS,),
        out_shape=(shape, shape, shape),
        in_specs=[
            pl.BlockSpec(memory_space=pltpu.SMEM),
            wide,
            whole((TOK, NS)),
            whole((TOK, NS)),
            whole((TOK, NH)),
            wide,
            wide,
            whole((TOK, NS)),
            whole((TOK, NH)),
            pl.BlockSpec((LANES, NS), lambda c: (c, 0)),
            whole((1, NH)),
            whole((1, NH)),
        ],
        out_specs=(state, state, state),
        scratch_shapes=[
            pltpu.VMEM((TOK, 2 * NH), BF16),
            pltpu.VMEM((TOK, 2 * NH), BF16),
            pltpu.VMEM((NS, TOK), BF16),
            pltpu.VMEM((NS, TOK), BF16),
            pltpu.VMEM((TOK, 2 * NH), BF16),
            pltpu.VMEM((NS, 2 * NH), BF16),
            pltpu.VMEM((NS, TOK), BF16),
        ],
        compiler_params=pltpu.CompilerParams(vmem_limit_bytes=LIMIT),
        name="first",
    )(length, rx, rb, rc, rdt, gy, px, pb, pdt, ps, bias, alog)


def exchange_kernel(
    nz, nx, ny,
    fresh_ref, entry_ref, end_in, decay_ref, scale_ref,
    pre_out, suf_out, seed_out, end_out,
    pre, suf, fsend, bsend, seedc, ra, rb, sa, sb, ra2, rb2, own, rz, zfull, enda, endb, endown, seed, end,
    fs, fr, bs, br, s1, r1, s2, r2, s3, r3, s4, r4, s5, r5, s6, r6, e1s, e1r, e2s, e2r, e3s, e3r,
):
    dp, z, r = lax.axis_index("dp"), lax.axis_index("ctx"), lax.axis_index("resp")
    x, y = r // ny, lax.rem(r, ny)
    half = PAIRS // 2
    pa, pb = half // nx, half // ny
    qa, qb = pa // ny, pb // nx
    rows = NS // nz
    dev = lambda zz, xx, yy: (dp, zz, xx * ny + yy)
    xs = [lax.rem(x + i, nx) for i in range(1, nx)]
    ys = [lax.rem(y + i, ny) for i in range(1, ny)]
    zs = [lax.rem(z + i, nz) for i in range(1, nz)]

    barrier = pltpu.get_barrier_semaphore()
    partners = [dev(z, t, y) for t in xs] + [dev(z, x, t) for t in ys] + [dev(t, x, y) for t in zs]
    for partner in partners:
        pl.semaphore_signal(barrier, inc=1, device_id=partner, device_id_type=MESH)

    def scale(q, carry):
        seedc[q] = entry_ref[q] * scale_ref[q]
        return carry

    lax.fori_loop(0, PAIRS, scale, 0)

    @pl.when(z == 0)
    def _():
        pre[...] = jnp.zeros_like(pre)

    @pl.when(z == nz - 1)
    def _():
        suf[...] = jnp.zeros_like(suf)

    pl.semaphore_wait(barrier, len(partners))

    def copy(src, dst, send, recv, to):
        return pltpu.make_async_remote_copy(
            src_ref=src, dst_ref=dst, send_sem=send, recv_sem=recv, device_id=to, device_id_type=MESH
        )

    def phase1():
        return [
            copy(seedc.at[pl.ds(t * pa, pa)], ra.at[i], s1.at[i], r1.at[i], dev(z, t, y))
            for i, t in enumerate(xs)
        ] + [
            copy(seedc.at[pl.ds(half + t * pb, pb)], rb.at[i], s1.at[nx + i], r1.at[nx + i], dev(z, x, t))
            for i, t in enumerate(ys)
        ]

    def phase2():
        return [
            copy(sa.at[pl.ds(t * qa, qa)], ra2.at[i], s2.at[i], r2.at[i], dev(z, x, t))
            for i, t in enumerate(ys)
        ] + [
            copy(sb.at[pl.ds(t * qb, qb)], rb2.at[i], s2.at[ny + i], r2.at[ny + i], dev(z, t, y))
            for i, t in enumerate(xs)
        ]

    def phase3():
        return [
            copy(own.at[:, pl.ds(t * rows, rows)], rz.at[i], s3.at[i], r3.at[i], dev(t, x, y))
            for i, t in enumerate(zs)
        ]

    def phase4():
        mine = zfull.at[:, pl.ds(z * rows, rows)]
        return [copy(mine, mine, s4.at[i], r4.at[i], dev(t, x, y)) for i, t in enumerate(zs)]

    la, lb = x * pa + y * qa, half + y * pb + x * qb

    def phase5():
        found = []
        for k, whole in enumerate((seed, end)):
            for i, t in enumerate(ys):
                at = k * (nx + ny) + i
                found.append(
                    copy(zfull.at[pl.ds(k * (qa + qb), qa)], whole.at[pl.ds(la, qa)], s5.at[at], r5.at[at], dev(z, x, t))
                )
            for i, t in enumerate(xs):
                at = k * (nx + ny) + ny + i
                found.append(
                    copy(zfull.at[pl.ds(k * (qa + qb) + qa, qb)], whole.at[pl.ds(lb, qb)], s5.at[at], r5.at[at], dev(z, t, y))
                )
        return found

    def phase6():
        found = []
        for k, whole in enumerate((end, seed)):
            for i, t in enumerate(xs):
                at = k * (nx + ny) + i
                mine = whole.at[pl.ds(x * pa, pa)]
                found.append(copy(mine, mine, s6.at[at], r6.at[at], dev(z, t, y)))
            for i, t in enumerate(ys):
                at = k * (nx + ny) + nx + i
                mine = whole.at[pl.ds(half + y * pb, pb)]
                found.append(copy(mine, mine, s6.at[at], r6.at[at], dev(z, x, t)))
        return found

    on_plane = z == nz - 1
    on_x, on_y = on_plane & (x == nx - 1), on_plane & (y == ny - 1)
    source = on_x & on_y

    def end1():
        return [
            copy(end_in.at[pl.ds(t * pa, pa)], enda, e1s.at[i], e1r.at[0], dev(z, t, y)) for i, t in enumerate(xs)
        ] + [
            copy(end_in.at[pl.ds(half + t * pb, pb)], endb, e1s.at[nx + i], e1r.at[1], dev(z, x, t))
            for i, t in enumerate(ys)
        ]

    def end2a():
        return [
            copy(enda.at[pl.ds(t * qa, qa)], endown.at[pl.ds(0, qa)], e2s.at[i], e2r.at[0], dev(z, x, t))
            for i, t in enumerate(ys)
        ]

    def end2b():
        return [
            copy(endb.at[pl.ds(t * qb, qb)], endown.at[pl.ds(qa, qb)], e2s.at[ny + i], e2r.at[1], dev(z, t, y))
            for i, t in enumerate(xs)
        ]

    def end3():
        return [
            copy(
                endown.at[:, pl.ds(t * rows, rows)], zfull.at[pl.ds(qa + qb, qa + qb), pl.ds(t * rows, rows)],
                e3s.at[i], e3r.at[0], dev(t, x, y),
            )
            for i, t in enumerate(zs)
        ]

    def start(copies):
        for one in copies:
            one.start()

    def wait_send(copies):
        for one in copies:
            one.wait_send()

    def wait_recv(copies):
        for one in copies:
            one.wait_recv()

    def do1():
        start(phase1())

        @pl.when(source)
        def _():
            start(end1())

    def do2():
        wait_recv(phase1())
        for q in range(pa):
            total = seedc[x * pa + q]
            for i in range(nx - 1):
                total = total + ra[i, q]
            sa[q] = total
        for q in range(pb):
            total = seedc[half + y * pb + q]
            for i in range(ny - 1):
                total = total + rb[i, q]
            sb[q] = total
        start(phase2())

        @pl.when(source)
        def _():
            enda[...] = end_in[pl.ds(x * pa, pa)]
            endb[...] = end_in[pl.ds(half + y * pb, pb)]

        @pl.when(on_y)
        def _():
            @pl.when(x != nx - 1)
            def _():
                end1()[0].wait_recv()

            start(end2a())
            for q in range(qa):
                endown[q] = enda[y * qa + q]

        @pl.when(on_x)
        def _():
            @pl.when(y != ny - 1)
            def _():
                end1()[nx - 1].wait_recv()

            start(end2b())
            for q in range(qb):
                endown[qa + q] = endb[x * qb + q]

    def do3():
        wait_recv(phase2())
        for q in range(qa):
            total = sa[y * qa + q]
            for i in range(ny - 1):
                total = total + ra2[i, q]
            own[q] = total
        for q in range(qb):
            total = sb[x * qb + q]
            for i in range(nx - 1):
                total = total + rb2[i, q]
            own[qa + q] = total
        start(phase3())

        @pl.when(on_plane)
        def _():
            @pl.when(y != ny - 1)
            def _():
                end2a()[0].wait_recv()

            @pl.when(x != nx - 1)
            def _():
                end2b()[0].wait_recv()

            start(end3())
            mine = pl.ds(z * rows, rows)
            for q in range(qa + qb):
                zfull[qa + qb + q, mine] = endown[q, mine]

    def do4():
        wait_recv(phase3())
        mine = pl.ds(z * rows, rows)
        for q in range(qa + qb):
            total = own[q, mine]
            for i in range(nz - 1):
                total = total + rz[i, q]
            zfull[q, mine] = total

        @pl.when(jnp.logical_not(on_plane))
        def _():
            end3()[0].wait_recv()

        start(phase4())

    def do5():
        wait_recv(phase4())
        start(phase5())
        for k, whole in enumerate((seed, end)):
            for q in range(qa):
                whole[la + q] = zfull[k * (qa + qb) + q]
            for q in range(qb):
                whole[lb + q] = zfull[k * (qa + qb) + qa + q]

    def do6():
        wait_recv(phase5())
        start(phase6())

    def do7():
        wait_recv(phase6())
        for phase in (phase1, phase2, phase3, phase4, phase5, phase6):
            wait_send(phase())

        @pl.when(source)
        def _():
            wait_send(end1())

        @pl.when(on_y)
        def _():
            wait_send(end2a())

        @pl.when(on_x)
        def _():
            wait_send(end2b())

        @pl.when(on_plane)
        def _():
            wait_send(end3())

    piece = 1
    count = PAIRS // piece

    def forward(c):
        at = pl.ds(c * piece, piece)
        return copy(fsend.at[at], pre.at[at], fs.at[c], fr.at[c], dev(lax.rem(z + 1, nz), x, y))

    def backward(c):
        at = pl.ds(c * piece, piece)
        return copy(bsend.at[at], suf.at[at], bs.at[c], br.at[c], dev(lax.rem(z + nz - 1, nz), x, y))

    def step(i, carry):
        cf = i - z

        @pl.when((cf >= 0) & (cf < count))
        def _():
            @pl.when(z > 0)
            def _():
                forward(cf).wait_recv()

            @pl.when(z < nz - 1)
            def _():
                at = pl.ds(cf * piece, piece)
                fsend[at] = decay_ref[at] * pre[at] + fresh_ref[at]
                forward(cf).start()

        cb = i - (nz - 1 - z)

        @pl.when((cb >= 0) & (cb < count))
        def _():
            @pl.when(z < nz - 1)
            def _():
                backward(cb).wait_recv()

            @pl.when(z > 0)
            def _():
                at = pl.ds(cb * piece, piece)
                bsend[at] = decay_ref[at] * suf[at] + entry_ref[at]
                backward(cb).start()

        return carry

    total = count + nz - 1
    do1()
    marks = [total * k // 7 for k in range(1, 6)]
    done = 0
    for mark, act in zip(marks, (do2, do3, do4, do5, do6)):
        lax.fori_loop(done, mark, step, 0)
        act()
        done = mark
    lax.fori_loop(done, total, step, 0)
    do7()

    def finish(c, carry):
        @pl.when(z < nz - 1)
        def _():
            forward(c).wait_send()

        @pl.when(z > 0)
        def _():
            backward(c).wait_send()

        return carry

    lax.fori_loop(0, count, finish, 0)
    pre_out[...] = pre[...]
    suf_out[...] = suf[...]
    seed_out[...] = seed[...]
    end_out[...] = end[...]


def factors(count):
    first = 1
    while first * first < count:
        first *= 2
    return first, count // first


def exchange_call(mesh_shape, fresh, entry, end, decay, scale):
    nz = mesh_shape["ctx"]
    nx, ny = factors(mesh_shape["resp"])
    half = PAIRS // 2
    pa, pb = half // nx, half // ny
    qa, qb = pa // ny, pb // nx
    rows = NS // nz
    shape = jax.ShapeDtypeStruct((PAIRS, NS, 128), F32)
    vmem = pl.BlockSpec(memory_space=pltpu.VMEM)
    buf = lambda *lead: pltpu.VMEM(lead + (128,), F32)
    sem = lambda n: pltpu.SemaphoreType.DMA((n,))
    return pl.pallas_call(
        functools.partial(exchange_kernel, nz, nx, ny),
        out_shape=(shape,) * 4,
        in_specs=[vmem] * 5,
        out_specs=(vmem,) * 4,
        scratch_shapes=[buf(PAIRS, NS)] * 5
        + [
            buf(nx - 1, pa, NS),
            buf(ny - 1, pb, NS),
            buf(pa, NS),
            buf(pb, NS),
            buf(ny - 1, qa, NS),
            buf(nx - 1, qb, NS),
            buf(qa + qb, NS),
            buf(nz - 1, qa + qb, rows),
            buf(2 * (qa + qb), NS),
            buf(pa, NS),
            buf(pb, NS),
            buf(qa + qb, NS),
            buf(PAIRS, NS),
            buf(PAIRS, NS),
        ]
        + [sem(PAIRS)] * 4
        + [sem(nx + ny)] * 4
        + [sem(nz)] * 4
        + [sem(2 * (nx + ny))] * 4
        + [sem(nx + ny), sem(2), sem(nx + ny), sem(2), sem(nz), sem(1)],
        compiler_params=pltpu.CompilerParams(collective_id=0, has_side_effects=True, vmem_limit_bytes=LIMIT),
        name="exchange",
    )(fresh, entry, end, decay, scale)


def last_kernel(
    len_ref, fac_ref, rx_ref, rb_ref, rc_ref, rdt_ref, gy_ref, px_ref, pb_ref, pdt_ref, ps_ref, bias_ref, alog_ref,
    skip_ref, pre_ref, suf_ref, end_ref, seed_ref, scan_ref, follow_ref,
    pdx_ref, pdb_ref, pdd_ref, rdx_ref, rdb_ref, rdc_ref, rdd_ref, small_ref,
    a_ch, d_ch, a_t, gt, dgt, dcat, wcat, ecat, e_in, r_in, d_in, z_in, row, acc1, acc2, acc3, inner, outer,
    pwcat, pr, pd, pz, pacc, pinner,
):
    c = pl.program_id(0)
    mask = row_mask(len_ref)

    @pl.when(c == 0)
    def _():
        bias, alog = bias_ref[...], alog_ref[...]
        z, d, _, a = steps(rdt_ref[...], bias, alog)
        z_in[...] = z
        d_in[...] = d
        at = a.T
        for k in range(CHUNKS):
            a_ch[k] = a[:, k * PER : k * PER + PER]
            d_ch[k] = d[:, k * PER : k * PER + PER]
            a_t[k] = at[k * PER : k * PER + PER]
        e = jnp.exp(a)
        r = jnp.exp(a[TOK - 1 :, :] - a)
        e_in[...] = e
        r_in[...] = r
        dcat[...] = cat2(d)
        wcat[...] = cat2(r * d)
        ecat[...] = cat2(e)
        scores = nt(rb_ref[...], rc_ref[...])
        gt[...] = jnp.where(iota((TOK, TOK), 0) <= iota((TOK, TOK), 1), scores, 0.0)
        dgt[...] = jnp.zeros_like(dgt)
        for acc in (acc1, acc2, acc3, inner, outer, pacc, pinner, rdb_ref, rdc_ref, pdb_ref):
            acc[...] = jnp.zeros_like(acc)
        z, d, _, a = steps(pdt_ref[...], bias, alog)
        pz[...] = z
        pd[...] = d
        r = jnp.exp(a[TOK - 1 :, :] - a)
        pr[...] = r
        pwcat[...] = cat2(r * d)

    spread2 = spreader(c, 2 * NH)
    spread = spread2[:NH]
    both = lambda ref: jnp.concatenate([ref[0], ref[1]], axis=1)

    x = rx_ref[...]
    gy = (gy_ref[...].astype(F32) * mask).astype(BF16)
    xf, gf = x.astype(F32), gy.astype(F32)
    lane = iota((1, 128), 1) < HD
    q1 = []
    for pair in range(2):
        xp, gp = x[:, pair * 128 : pair * 128 + 128], gy[:, pair * 128 : pair * 128 + 128]
        total = [None] * 4
        for odd in range(2):
            j = 2 * pair + odd
            own = jnp.logical_not(lane) if odd else lane
            xh = jnp.where(own, xp, jnp.zeros_like(xp))
            gh = jnp.where(own, gp, jnp.zeros_like(gp))
            col, dcol, arow = a_ch[c, :, j : j + 1], d_ch[c, :, j : j + 1], a_t[c, j : j + 1, :]
            rows = [None, None]
            for b in range(4):
                s0 = b * 64
                t0 = (b // 2) * 128
                sl = slice(s0, s0 + 64)
                g = gt[sl, t0:]
                decay = jnp.exp(jnp.minimum(arow[:, t0:] - col[sl], 0.0))
                hi, lo = split2(decay * g)
                gpart = gh[t0:]
                q = nn(hi, gpart) + nn(lo, gpart)
                total[b] = q if total[b] is None else total[b] + q
                k = decay * nt(xh[sl], gpart) * dcol[sl]
                dgt[sl, t0:] += k
                part = jnp.sum(k * g, axis=0, keepdims=True)
                at = b // 2
                rows[at] = part if rows[at] is None else rows[at] + part
            row[c, j : j + 1, :] = rows[0]
            row[c, j : j + 1, 128:] += rows[1]
        q1.append(jnp.concatenate(total, axis=0))
    q1 = jnp.concatenate(q1, axis=1)
    factor = fac_ref[0, 0]
    state = scan_ref[0] * both(end_ref) + both(pre_ref)
    grad = both(suf_ref)
    shi, slo = split2(state)
    ghi, glo = split2(grad)
    rb, rc = rb_ref[...], rc_ref[...]
    q2 = nn(rb, ghi) + nn(rb, glo)
    cs = nn(rc, shi) + nn(rc, slo)
    wide_w = nn(wcat[...], spread2)
    rdx_ref[...] = (factor * (nn(dcat[...], spread2) * q1 + wide_w * q2 + skip_ref[0] * gf)).astype(BF16)
    acc1[...] += by_head(xf * q1, spread)
    acc2[...] += by_head(xf * q2, spread)
    acc3[...] += by_head(gf * cs, spread)
    whi, wlo = split2(wide_w * xf)
    rdb_ref[...] += nt(whi, ghi) + (nt(wlo, ghi) + nt(whi, glo))
    ehi, elo = split2(nn(ecat[...], spread2) * gf)
    rdc_ref[...] += nt(ehi, shi) + (nt(elo, shi) + nt(ehi, slo))
    inner[...] += by_head(fold8(state * grad), spread)
    outer[...] += by_head(fold8(xf * gf), spread)

    pxf = px_ref[...].astype(F32)
    pgrad = follow_ref[0] * both(seed_ref)
    ghi, glo = split2(pgrad)
    pb = pb_ref[...]
    q2 = nn(pb, ghi) + nn(pb, glo)
    wide_w = nn(pwcat[...], spread2)
    pdx_ref[...] = (wide_w * q2).astype(BF16)
    pacc[...] += by_head(pxf * q2, spread)
    whi, wlo = split2(wide_w * pxf)
    pdb_ref[...] += nt(whi, ghi) + (nt(wlo, ghi) + nt(whi, glo))
    eye = jnp.where(iota((NS, NS), 0) == iota((NS, NS), 1), 1.0, 0.0).astype(BF16)
    pinner[...] += by_head(fold8(nt(eye, ps_ref[...]) * pgrad), spread)

    @pl.when(c == CHUNKS - 1)
    def _():
        rate = -jnp.exp(alog_ref[...])

        def close(z, d, r, dstep, da, last):
            cum = exact_nn(upper(), da) + last
            ddt = (dstep + rate * cum) / (1.0 + jnp.exp(-z))
            return ddt, cum * (rate * d)

        column = lambda v: jnp.sum(v, axis=0, keepdims=True)
        d, r, e = d_in[...], r_in[...], e_in[...]
        dstep = acc1[...] + r * acc2[...]
        erow = jnp.concatenate([row[k] for k in range(CHUNKS)], axis=0).T
        da = erow + e * acc3[...] - d * dstep
        last = e[TOK - 1 :] * column(inner[...]) + column(r * d * acc2[...])
        ddt, dalog = close(z_in[...], d, r, dstep, da, last)
        ddt = factor * ddt
        rdd_ref[...] = ddt
        bias_sum, alog_sum = column(ddt), factor * column(dalog)
        skip_sum = factor * column(outer[...])
        keep = jnp.where(iota((TOK, TOK), 0) <= iota((TOK, TOK), 1), dgt[...], 0.0)
        hi, lo = split2(keep)
        rdb_ref[...] = factor * (rdb_ref[...] + (nn(hi, rc) + nn(lo, rc)))
        hi, lo = split2(keep.T)
        rdc_ref[...] = factor * (rdc_ref[...] + (nn(hi, rb) + nn(lo, rb)))

        d, r = pd[...], pr[...]
        dstep = r * pacc[...]
        weighted = d * dstep
        last_decay = jnp.exp(column(rate * d))
        last = last_decay * column(pinner[...]) + column(weighted)
        ddt, dalog = close(pz[...], d, r, dstep, -weighted, last)
        pdd_ref[...] = ddt
        small_ref[0:1] = bias_sum + column(ddt)
        small_ref[1:2] = alog_sum + column(dalog)
        small_ref[2:3] = skip_sum


def last_call(length, factor, rx, rb, rc, rdt, gy, px, pb, pdt, ps, bias, alog, skip, pre, suf, end, seed, scan, follow):
    wide = pl.BlockSpec((TOK, LANES), lambda c: (0, c))
    whole = lambda *shape: pl.BlockSpec(shape, lambda c: (0,) * len(shape))
    state = pl.BlockSpec((2, NS, 128), lambda c: (c, 0, 0))
    lanes = pl.BlockSpec((1, 1, LANES), lambda c: (c, 0, 0))
    smem = pl.BlockSpec(memory_space=pltpu.SMEM)
    out = jax.ShapeDtypeStruct
    v = lambda *shape: pltpu.VMEM(shape, F32)
    b = lambda *shape: pltpu.VMEM(shape, BF16)
    return pl.pallas_call(
        last_kernel,
        grid=(CHUNKS,),
        out_shape=(
            out((TOK, NH * HD), BF16),
            out((TOK, NS), F32),
            out((TOK, NH), F32),
            out((TOK, NH * HD), BF16),
            out((TOK, NS), F32),
            out((TOK, NS), F32),
            out((TOK, NH), F32),
            out((3, NH), F32),
        ),
        in_specs=[
            smem, smem, wide, whole(TOK, NS), whole(TOK, NS), whole(TOK, NH), wide, wide, whole(TOK, NS), whole(TOK, NH),
            pl.BlockSpec((LANES, NS), lambda c: (c, 0)), whole(1, NH), whole(1, NH), lanes,
            state, state, state, state, lanes, lanes,
        ],
        out_specs=(
            wide, whole(TOK, NS), whole(TOK, NH), wide, whole(TOK, NS), whole(TOK, NS), whole(TOK, NH), whole(3, NH),
        ),
        scratch_shapes=[
            v(CHUNKS, TOK, PER), v(CHUNKS, TOK, PER), v(CHUNKS, PER, TOK), v(TOK, TOK), v(TOK, TOK),
            b(TOK, 2 * NH), b(TOK, 2 * NH), b(TOK, 2 * NH),
            v(TOK, NH), v(TOK, NH), v(TOK, NH), v(TOK, NH), v(CHUNKS, PER, TOK),
            v(TOK, NH), v(TOK, NH), v(TOK, NH), v(8, NH), v(8, NH),
            b(TOK, 2 * NH), v(TOK, NH), v(TOK, NH), v(TOK, NH), v(TOK, NH), v(8, NH),
        ],
        compiler_params=pltpu.CompilerParams(vmem_limit_bytes=LIMIT),
        name="last",
    )(length, factor, rx, rb, rc, rdt, gy, px, pb, pdt, ps, bias, alog, skip, pre, suf, end, seed, scan, follow)


def body(
    mesh_shape,
    prompt_x, prompt_b, prompt_dt, prompt_states, resp_x, resp_b, resp_c, resp_dt, grad_out, lengths, advantages,
    dt_bias, a_log, skip,
):
    nz, nr = mesh_shape["ctx"], mesh_shape["resp"]
    px, pb, pdt = prompt_x[0], prompt_b[0], prompt_dt[0]
    ps = prompt_states.reshape(NH * HD, NS)
    rx, rb, rc, rdt, gy = resp_x[0, 0], resp_b[0, 0], resp_c[0, 0], resp_dt[0, 0], grad_out[0, 0]
    bias, alog = dt_bias[None], a_log[None]

    def block_decay(dt):
        return jnp.exp(jnp.sum(-jnp.exp(alog) * jax.nn.softplus(dt + bias), axis=0))

    own_decay = block_decay(rdt)
    decays = jnp.stack([own_decay, block_decay(pdt)])
    every = lax.all_gather(decays, ("ctx", "resp"))
    here, row = lax.axis_index("ctx"), lax.axis_index("resp")
    of_resp = lax.dynamic_index_in_dim(every[:, 0].reshape(nz, nr, NH), row, 1, keepdims=False)
    scan = jnp.prod(jnp.where((jnp.arange(nz) < here)[:, None], of_resp, 1.0), axis=0)
    later = (jnp.arange(nz * nr) > here * nr + row)[:, None]
    follow = jnp.prod(jnp.where(later, every[:, 1], 1.0), axis=0)
    length = lengths
    factor = advantages * float(nz * TOK) / lengths.astype(F32)

    lanes = lambda v: jnp.repeat(v, HD).reshape(CHUNKS, 1, LANES)
    pairs = lambda v: jnp.repeat(v, HD).reshape(PAIRS, 1, 128)

    fresh, entry, end = first_call(length, rx, rb, rc, rdt, gy, px, pb, pdt, ps, bias, alog)
    pre, suf, seed, end = exchange_call(
        mesh_shape, fresh, entry, end, pairs(own_decay), pairs(scan * factor[0, 0])
    )
    pdx, pdb, pdd, rdx, rdb, rdc, rdd, small = last_call(
        length, factor, rx, rb, rc, rdt, gy, px, pb, pdt, ps, bias, alog, lanes(skip),
        pre, suf, end, seed, lanes(scan), lanes(follow),
    )
    small = lax.psum(small, ("dp", "ctx", "resp"))
    return (
        pdx[None], pdb[None], pdd[None], rdx[None, None], rdb[None, None], rdc[None, None], rdd[None, None],
        small[0], small[1], small[2],
    )


def solution(mesh):
    wide = P("dp", ("ctx", "resp"), None)
    long = P("dp", "resp", "ctx", None)
    in_specs = (
        wide, wide, wide, P("dp", ("ctx", "resp"), None, None, None), long, long, long, long, long,
        P("dp", "resp"), P("dp", "resp"), P(), P(), P(),
    )
    out_specs = (wide, wide, wide, long, long, long, long, P(), P(), P())
    return jax.shard_map(
        functools.partial(body, dict(mesh.shape)), mesh=mesh, in_specs=in_specs, out_specs=out_specs, check_vma=False
    )
```

time: 1220 us -> 629 us (0.52); the launches traced: 1200 us -> 628 us
  other arithmetic: 261 us -> 1.75 us
  waiting for transfers between devices: 234 us -> 0 us
  matrix products: 174 us -> 0 us
  Pallas kernels: 0 us -> 167 us
  local copies, waits for them, and re-layouts: 111 us -> 10.8 us
  blocking collectives: 392 us -> 447 us
  between operations: 17.5 us -> 2.1 us
  loops' own time: 12.7 us -> 0 us
    psum x2 -> x0, waiting for transfers between devices: 234 us -> none  [the longest x1 123 us: body(): seed_grad = lax.psum(start_grad, ('ctx', 'resp'))]
    dot_general x48 -> x0, matrix products: 174 us -> none  [the longest x18 61.6 us: block_state(): jnp.einsum('shp,sn->hpn', driven, b_proj, precision=precise)]
    pallas_call x0 -> x3, Pallas kernels: none -> 167 us  [the longest x1 111 us: exchange_call(): pl.pallas_call(functools.partial(exchange_kernel, nz, nx, ny), out_shape=...]
    select_n x154 -> x0, other arithmetic: 139 us -> none  [the longest x152 135 us: turn(): return jax.tree.map(lambda a, b: jnp.where(reached, a, b), new, before)]
    psum x1, blocking collectives: 79.1 us -> 153 us  [body(): small = lax.psum(small, ('dp', 'ctx', 'resp'))]
    another operation x70 -> x0, other arithmetic: 48.7 us -> none
    another operation x93 -> x0, local copies, waits for them, and re-layouts: 32.6 us -> none
    dynamic_update_slice x24 -> x0, local copies, waits for them, and re-layouts: 26.7 us -> none  [response_grads(): lax.map(response_per_block, (by_heads(inputs, blocks), by_heads(raw_step,...]
  transfers between devices with their start and end apart: 4 -> 0, of which waited for: 2 -> 0; matrix products, arithmetic and copies ran while one was open for 15% -> 0% of each run, Pallas kernels for 0% -> 0%
where the time goes in v1:
time: 629 us; the launch traced here: 628 us
  blocking collectives  447 us (71%)
  Pallas kernels  167 us (27%)
  local copies, waits for them, and re-layouts  10.8 us (2%)
    all_gather x1, blocking collectives, body(): every = lax.all_gather(decays, ('ctx', 'resp'))  294 us
    psum x1, blocking collectives, body(): small = lax.psum(small, ('dp', 'ctx', 'resp'))  153 us
    pallas_call x1, Pallas kernels, exchange_call(): pl.pallas_call(functools.partial(exchange_kernel, nz, nx, ny), out_shape=...  111 us
    pallas_call x1, Pallas kernels, last_call(): pl.pallas_call(last_kernel, grid=(CHUNKS,), out_shape=(out((TOK, NH * HD)...  39.9 us
    pallas_call x1, Pallas kernels, first_call(): pl.pallas_call(first_kernel, grid=(CHUNKS,), out_shape=(shape, shape, sha...  15.3 us

profile of v1, /device:TPU:1, one launch (start us, length us, event | category | flops | bytes accessed | tf_op | source)
XLA Modules:
  0.0 628.2 jit_solution(9666908027518632741)
XLA Ops:
  2.0 0.7 exponential_negate_fusion
  2.7 0.7 broadcast_in_dim.86
  3.4 0.1 broadcast_in_dim.87
  3.5 0.7 broadcast_in_dim.88.skip_ref
  4.2 0.9 copy.33
  5.1 1.0 copy.32
  6.1 0.0 copy-start.1
  6.1 0.9 fusion.3
  7.0 0.1 exp.45
  7.2 0.1 broadcast_in_dim.89
  7.3 0.7 broadcast_in_dim.90.decay_ref
  8.0 293.9 %all-gather.1 = f32[128,2,64]{2,1,0:T(2,128)S(1)} all-gather(f32[1,2,64]{2,1,0:T(2,128)S(1)} %maximum_bitcast_fusion), channel_id=2, replica_groups=mesh['dp'=2,'ctx'=8,'resp'=16] {'ctx','resp'}, dimensions={0}, use_global_device_ids=true | all-gather | bytes 66048 | tf_op jit(solution)/shard_map/all_gather | solution.py:784
  301.9 0.1 fusion.4
  302.0 0.1 select_reduce_fusion
  302.1 0.1 select_reduce_fusion.1
  302.2 0.1 broadcast_in_dim.95
  302.3 0.1 broadcast_in_dim.100
  302.4 0.1 mul.36
  302.5 0.1 broadcast_in_dim.93
  302.6 0.7 broadcast_in_dim.94.scale_ref
  303.3 0.1 broadcast_in_dim.101
  303.4 0.7 broadcast_in_dim.102.follow_ref
  304.1 0.1 broadcast_in_dim.96
  304.2 0.7 broadcast_in_dim.97.scan_ref
  304.9 0.0 copy-done.1
  304.9 15.3 %first.1 = (f32[32,128,128]{2,1,0:T(8,128)}, f32[32,128,128]{2,1,0:T(8,128)}, f32[32,128,128]{2,1,0:T(8,128)}) custom-call(s32[1,1]{1,0:T(1,128)S(6)} %copy.36.len_ref, bf16[256,4096]{1,0:T(8,128)(2,1)} %bitcast.36, bf16[256,128]{1,0:T(8,128)(2,1)} %bitcast.48, bf16[256,128]{1,0:T(8,128)(2,1)} %bitcast.50, f32[256,64]{1,0:T(8,128)} %bitcast.46, ...), custom_call_target="tpu_custom_call" | custom-call | tf_op jit(solution)/shard_map/first/pallas_call | solution.py:152
  320.2 111.5 %exchange.1 = (f32[32,128,128]{2,1,0:T(8,128)}, f32[32,128,128]{2,1,0:T(8,128)}, f32[32,128,128]{2,1,0:T(8,128)}, f32[32,128,128]{2,1,0:T(8,128)}) custom-call(f32[32,128,128]{2,1,0:T(8,128)} %get-tuple-element.25.fresh_ref, f32[32,128,128]{2,1,0:T(8,128)} %get-tuple-element.26.entry_ref, f32[32,128,128]{2,1,0:T(8,128)} %get-tuple-element.27.end_in, ...), custom_call_target="tpu_custom_call" | custom-call | tf_op jit(solution)/shard_map/exchange/pallas_call | solution.py:545
  431.7 39.9 %last.1 = (bf16[256,4096]{1,0:T(8,128)(2,1)}, f32[256,128]{1,0:T(8,128)}, f32[256,64]{1,0:T(8,128)}, bf16[256,4096]{1,0:T(8,128)(2,1)}, f32[256,128]{1,0:T(8,128...) custom-call(s32[1,1]{1,0:T(1,128)S(6)} %copy.36.len_ref, f32[1,1]{1,0:T(1,128)} %div.3.fac_ref, ...), custom_call_target="tpu_custom_call" | custom-call | tf_op jit(solution)/shard_map/last/pallas_call | solution.py:735
  471.6 152.8 %psum.7 = f32[3,64]{1,0:T(4,128)S(1)} all-reduce(f32[3,64]{1,0:T(4,128)} %get-tuple-element.39), channel_id=1, replica_groups=mesh['dp'=2,'ctx'=8,'resp'=16] {'dp','ctx','resp'}, use_global_device_ids=true, to_apply=%region_4.5 | all-reduce | flops 192 | bytes 1536 | tf_op jit(solution)/shard_map/psum | solution.py:804
  624.4 0.5 slice_bitcast_fusion
  624.9 1.6 copy.34
  626.6 1.6 copy.35
  (9 shorter events, 0.1 us)
Async XLA Ops:
  5.1 299.7 %copy-start = (f32[1,256,64]{2,1,0:T(8,128)}, f32[1,256,64]{2,1,0:T(8,128)S(1)}, u32[]{:S(2)}) copy-start(f32[1,256,64]{2,1,0:T(8,128)S(1)} %copy.33) | copy-start | bytes 196612
  6.1 298.7 %copy-start.1 = (f32[1,1,256,64]{3,2,1,0:T(8,128)}, f32[1,1,256,64]{3,2,1,0:T(8,128)S(1)}, u32[]{:S(2)}) copy-start(f32[1,1,256,64]{3,2,1,0:T(8,128)S(1)} %copy.32) | copy-start | bytes 196612

commit v2 on v1

v2 whole, which is shorter than its diff:
```python
import functools

import jax
import jax.numpy as jnp
from jax import lax
from jax.experimental import pallas as pl
from jax.experimental.pallas import tpu as pltpu
from jax.sharding import PartitionSpec as P

MESH = pl.DeviceIdType.MESH
F32 = jnp.float32
BF16 = jnp.bfloat16
TOK = 256
LANES = 256
PER = 4
NH = 64
HD = 64
NS = 128
CHUNKS = 16
PAIRS = 32
LIMIT = 56 * 1024 * 1024


def nn(a, b):
    return lax.dot_general(a, b, (((1,), (0,)), ((), ())), preferred_element_type=F32)


def nt(a, b):
    return lax.dot_general(a, b, (((1,), (1,)), ((), ())), preferred_element_type=F32)


def split2(v):
    hi = v.astype(BF16)
    return hi, (v - hi.astype(F32)).astype(BF16)


def split3(v):
    hi = v.astype(BF16)
    rest = v - hi.astype(F32)
    mid = rest.astype(BF16)
    return hi, mid, (rest - mid.astype(F32)).astype(BF16)


def exact_nn(tri, v):
    hi, mid, lo = split3(v)
    return nn(tri, hi) + (nn(tri, mid) + nn(tri, lo))


def iota(shape, dim):
    return lax.broadcasted_iota(jnp.int32, shape, dim)


def lower():
    return jnp.where(iota((TOK, TOK), 0) >= iota((TOK, TOK), 1), 1.0, 0.0).astype(BF16)


def upper():
    return jnp.where(iota((TOK, TOK), 0) <= iota((TOK, TOK), 1), 1.0, 0.0).astype(BF16)


def spreader(c, rows):
    head = iota((rows, LANES), 0) & (NH - 1)
    lane = iota((rows, LANES), 1) >> 6
    return jnp.where(head == lane + c * PER, 1.0, 0.0).astype(BF16)


def steps(dt, bias, alog):
    z = dt + bias
    d = jnp.maximum(z, 0.0) + jnp.log1p(jnp.exp(-jnp.abs(z)))
    rate = -jnp.exp(alog)
    a = exact_nn(lower(), rate * d)
    return z, d, rate, a


def cat2(v):
    hi, lo = split2(v)
    return jnp.concatenate([hi, lo], axis=1)


def by_head(v, spread):
    hi, lo = split2(v)
    return nt(hi, spread) + nt(lo, spread)


def fold8(v):
    total = v[0:8]
    for at in range(8, v.shape[0], 8):
        total = total + v[at : at + 8]
    return total


def cat3(v):
    return jnp.concatenate(split3(v), axis=1)


def column(v):
    return jnp.sum(v, axis=0, keepdims=True)


def triangle():
    return iota((TOK, TOK), 0) <= iota((TOK, TOK), 1)


def both(ref, c):
    return jnp.concatenate([ref[2 * c], ref[2 * c + 1]], axis=1)


def row_mask(length_ref):
    position = lax.axis_index("ctx") * TOK + iota((TOK, 1), 0)
    return jnp.where(position < length_ref[0, 0], 1.0, 0.0)


def first_kernel(
    len_ref, rx_ref, rb_ref, rc_ref, rdt_ref, gy_ref, px_ref, pb_ref, pdt_ref, ps_ref, bias_ref, alog_ref,
    fresh_ref, entry_ref, end_ref, decay_ref,
    wcat, ecat, bt, ct, pwcat, pecat, pbt,
):
    c = pl.program_id(0)
    last = (lax.axis_index("ctx") == lax.axis_size("ctx") - 1) & (
        lax.axis_index("resp") == lax.axis_size("resp") - 1
    )

    @pl.when(c == 0)
    def _():
        bias, alog = bias_ref[...], alog_ref[...]
        _, d, _, a = steps(rdt_ref[...], bias, alog)
        wcat[...] = cat2(jnp.exp(a[TOK - 1 :, :] - a) * d)
        ecat[...] = cat2(jnp.exp(a) * row_mask(len_ref))
        bt[...] = rb_ref[...].astype(F32).T.astype(BF16)
        ct[...] = rc_ref[...].astype(F32).T.astype(BF16)
        decay_ref[...] = jnp.ones_like(decay_ref)
        decay_ref[0:1, :NH] = jnp.exp(a[TOK - 1 :, :])
        _, _, _, a = steps(pdt_ref[...], bias, alog)
        decay_ref[1:2, :NH] = jnp.exp(a[TOK - 1 :, :])

    @pl.when((c == 0) & last)
    def _():
        bias, alog = bias_ref[...], alog_ref[...]
        _, d, _, a = steps(pdt_ref[...], bias, alog)
        pwcat[...] = cat2(jnp.exp(a[TOK - 1 :, :] - a) * d)
        pecat[...] = cat2(jnp.broadcast_to(jnp.exp(a[TOK - 1 :, :]), (NS, NH)))
        pbt[...] = pb_ref[...].astype(F32).T.astype(BF16)

    spread = spreader(c, 2 * NH)

    def put(ref, value):
        ref[0] = value[:, :128]
        ref[1] = value[:, 128:]

    hi, lo = split2(nn(wcat[...], spread) * rx_ref[...].astype(F32))
    put(fresh_ref, nn(bt[...], hi) + nn(bt[...], lo))
    hi, lo = split2(nn(ecat[...], spread) * gy_ref[...].astype(F32))
    put(entry_ref, nn(ct[...], hi) + nn(ct[...], lo))

    @pl.when(last)
    def _():
        hi, lo = split2(nn(pwcat[...], spread) * px_ref[...].astype(F32))
        eye = jnp.where(iota((NS, NS), 0) == iota((NS, NS), 1), 1.0, 0.0).astype(BF16)
        saved = nt(eye, ps_ref[...])
        put(end_ref, nn(pecat[...], spread) * saved + (nn(pbt[...], hi) + nn(pbt[...], lo)))

    @pl.when(jnp.logical_not(last))
    def _():
        end_ref[...] = jnp.zeros_like(end_ref)


def first_call(length, rx, rb, rc, rdt, gy, px, pb, pdt, ps, bias, alog):
    wide = pl.BlockSpec((TOK, LANES), lambda c: (0, c))
    whole = lambda shape: pl.BlockSpec(shape, lambda c: (0,) * len(shape))
    state = pl.BlockSpec((2, NS, 128), lambda c: (c, 0, 0))
    shape = jax.ShapeDtypeStruct((PAIRS, NS, 128), F32)
    return pl.pallas_call(
        first_kernel,
        grid=(CHUNKS,),
        out_shape=(shape, shape, shape, jax.ShapeDtypeStruct((8, 128), F32)),
        in_specs=[
            pl.BlockSpec(memory_space=pltpu.SMEM),
            wide,
            whole((TOK, NS)),
            whole((TOK, NS)),
            whole((TOK, NH)),
            wide,
            wide,
            whole((TOK, NS)),
            whole((TOK, NH)),
            pl.BlockSpec((LANES, NS), lambda c: (c, 0)),
            whole((1, NH)),
            whole((1, NH)),
        ],
        out_specs=(state, state, state, whole((8, 128))),
        scratch_shapes=[
            pltpu.VMEM((TOK, 2 * NH), BF16),
            pltpu.VMEM((TOK, 2 * NH), BF16),
            pltpu.VMEM((NS, TOK), BF16),
            pltpu.VMEM((NS, TOK), BF16),
            pltpu.VMEM((TOK, 2 * NH), BF16),
            pltpu.VMEM((NS, 2 * NH), BF16),
            pltpu.VMEM((NS, TOK), BF16),
        ],
        compiler_params=pltpu.CompilerParams(vmem_limit_bytes=LIMIT),
        name="first",
    )(length, rx, rb, rc, rdt, gy, px, pb, pdt, ps, bias, alog)


LAG = 3
MARKS = (1, 6, 8, 10, 13, 16)


def main_kernel(
    nz, nx, ny,
    len_ref, fac_ref, fresh_ref, entry_ref, end_in, tile_ref,
    rx_ref, rb_ref, rc_ref, rdt_ref, gy_ref, px_ref, pb_ref, pdt_ref, ps_ref, bias_ref, alog_ref, skip_ref,
    pdx_ref, pdb_ref, pdd_ref, rdx_ref, rdb_ref, rdc_ref, rdd_ref, small_ref,
    a_ch, d_ch, a_t, gt, dgt, q1_ref, dcat, wcat, ecat, e_in, r_in, d_in, z_in, row, acc1, acc2, acc3, inner, outer,
    pwcat, pr, pd, pz, pacc, pinner, scan_ref, fol_ref, lanes_ref,
    pre, suf, fsend, bsend, seedc, seed, end, ra, rb, sa, sb, ra2, rb2, own, rz, zfull, enda, endb, endown,
    tz, ty, tx, tp, mine_y, mine_x, sx, sy, sz, sd, terms,
    fs, fr, bs, br, s1, r1, s2, r2, s3, r3, s4, r4, s5, r5, s6, r6, e1s, e1r, e2s, e2r, e3s, e3r,
    tzs, tzr, tys, tyr, txs, txr, tps, tpr, xs_s, xs_r, ys_s, ys_r, zs_s, zs_r, ds_s, ds_r,
):
    dp, z, r = lax.axis_index("dp"), lax.axis_index("ctx"), lax.axis_index("resp")
    ndp = lax.axis_size("dp")
    x, y = r // ny, lax.rem(r, ny)
    half = PAIRS // 2
    pa, pb = half // nx, half // ny
    qa, qb = pa // ny, pb // nx
    rows = NS // nz
    dev = lambda zz, xx, yy: (dp, zz, xx * ny + yy)
    xs = [lax.rem(x + i, nx) for i in range(1, nx)]
    ys = [lax.rem(y + i, ny) for i in range(1, ny)]
    zs = [lax.rem(z + i, nz) for i in range(1, nz)]
    ds = [(lax.rem(dp + i, ndp), z, r) for i in range(1, ndp)]
    factor = fac_ref[0, 0]

    barrier = pltpu.get_barrier_semaphore()
    partners = [dev(z, t, y) for t in xs] + [dev(z, x, t) for t in ys] + [dev(t, x, y) for t in zs] + ds
    for partner in partners:
        pl.semaphore_signal(barrier, inc=1, device_id=partner, device_id_type=MESH)

    bias, alog = bias_ref[...], alog_ref[...]

    def prepare():
        zz, d, _, a = steps(rdt_ref[...], bias, alog)
        z_in[...] = zz
        d_in[...] = d
        at = a.T
        for k in range(CHUNKS):
            a_ch[k] = a[:, k * PER : k * PER + PER]
            d_ch[k] = d[:, k * PER : k * PER + PER]
            a_t[k] = at[k * PER : k * PER + PER]
        e = jnp.exp(a)
        rr = jnp.exp(a[TOK - 1 :, :] - a)
        e_in[...] = e
        r_in[...] = rr
        dcat[...] = cat2(d)
        wcat[...] = cat2(rr * d)
        ecat[...] = cat2(e)
        scores = nt(rb_ref[...], rc_ref[...])
        gt[...] = jnp.where(triangle(), scores, 0.0)
        dgt[...] = jnp.zeros_like(dgt)
        for acc in (acc1, acc2, acc3, inner, outer, pacc, pinner, rdb_ref, rdc_ref, pdb_ref):
            acc[...] = jnp.zeros_like(acc)
        zz, d, _, a = steps(pdt_ref[...], bias, alog)
        pz[...] = zz
        pd[...] = d
        rr = jnp.exp(a[TOK - 1 :, :] - a)
        pr[...] = rr
        pwcat[...] = cat2(rr * d)

    def to_lanes(v, c):
        return nn(cat3(v), spreader(c, 3 * NH))

    def put_lanes(v):
        def one(c, carry):
            wide = to_lanes(v, c)
            lanes_ref[2 * c] = wide[:, :128]
            lanes_ref[2 * c + 1] = wide[:, 128:]
            return carry

        lax.fori_loop(0, CHUNKS, one, 0)

    put_lanes(tile_ref[:, :NH])

    @pl.when(z == 0)
    def _():
        pre[...] = jnp.zeros_like(pre)

    @pl.when(z == nz - 1)
    def _():
        suf[...] = jnp.zeros_like(suf)

    pl.semaphore_wait(barrier, len(partners))

    def copy(src, dst, send, recv, to):
        return pltpu.make_async_remote_copy(
            src_ref=src, dst_ref=dst, send_sem=send, recv_sem=recv, device_id=to, device_id_type=MESH
        )

    def start(copies):
        for one in copies:
            one.start()

    def wait_send(copies):
        for one in copies:
            one.wait_send()

    def wait_recv(copies):
        for one in copies:
            one.wait_recv()

    def tiles_z():
        return [copy(tile_ref, tz.at[i], tzs.at[i], tzr.at[i], dev(t, x, y)) for i, t in enumerate(zs)]

    def tiles_y():
        return [copy(tile_ref, ty.at[i], tys.at[i], tyr.at[i], dev(z, x, t)) for i, t in enumerate(ys)]

    def tiles_x():
        return [copy(mine_y, tx.at[i], txs.at[i], txr.at[i], dev(z, t, y)) for i, t in enumerate(xs)]

    def tiles_p():
        return [copy(mine_x, tp.at[i], tps.at[i], tpr.at[i], dev(t, x, y)) for i, t in enumerate(zs)]

    def before(slots, at, size):
        total = jnp.ones((8, 128), F32)
        for i in range(size - 1):
            total = total * jnp.where(i + 1 <= at, slots[i], 1.0)
        return total

    def after(slots, at, size):
        total = jnp.ones((8, 128), F32)
        for i in range(size - 1):
            total = total * jnp.where(i + 1 > at, slots[i], 1.0)
        return total

    def phase1():
        return [
            copy(seedc.at[pl.ds(t * pa, pa)], ra.at[i], s1.at[i], r1.at[i], dev(z, t, y))
            for i, t in enumerate(xs)
        ] + [
            copy(seedc.at[pl.ds(half + t * pb, pb)], rb.at[i], s1.at[nx + i], r1.at[nx + i], dev(z, x, t))
            for i, t in enumerate(ys)
        ]

    def phase2():
        return [
            copy(sa.at[pl.ds(t * qa, qa)], ra2.at[i], s2.at[i], r2.at[i], dev(z, x, t))
            for i, t in enumerate(ys)
        ] + [
            copy(sb.at[pl.ds(t * qb, qb)], rb2.at[i], s2.at[ny + i], r2.at[ny + i], dev(z, t, y))
            for i, t in enumerate(xs)
        ]

    def phase3():
        return [
            copy(own.at[:, pl.ds(t * rows, rows)], rz.at[i], s3.at[i], r3.at[i], dev(t, x, y))
            for i, t in enumerate(zs)
        ]

    def phase4():
        mine = zfull.at[:, pl.ds(z * rows, rows)]
        return [copy(mine, mine, s4.at[i], r4.at[i], dev(t, x, y)) for i, t in enumerate(zs)]

    la, lb = x * pa + y * qa, half + y * pb + x * qb

    def phase5():
        found = []
        for k, whole in enumerate((seed, end)):
            for i, t in enumerate(ys):
                at = k * (nx + ny) + i
                found.append(
                    copy(zfull.at[pl.ds(k * (qa + qb), qa)], whole.at[pl.ds(la, qa)], s5.at[at], r5.at[at], dev(z, x, t))
                )
            for i, t in enumerate(xs):
                at = k * (nx + ny) + ny + i
                found.append(
                    copy(zfull.at[pl.ds(k * (qa + qb) + qa, qb)], whole.at[pl.ds(lb, qb)], s5.at[at], r5.at[at], dev(z, t, y))
                )
        return found

    def phase6():
        found = []
        for k, whole in enumerate((end, seed)):
            for i, t in enumerate(xs):
                at = k * (nx + ny) + i
                mine = whole.at[pl.ds(x * pa, pa)]
                found.append(copy(mine, mine, s6.at[at], r6.at[at], dev(z, t, y)))
            for i, t in enumerate(ys):
                at = k * (nx + ny) + nx + i
                mine = whole.at[pl.ds(half + y * pb, pb)]
                found.append(copy(mine, mine, s6.at[at], r6.at[at], dev(z, x, t)))
        return found

    on_plane = z == nz - 1
    on_x, on_y = on_plane & (x == nx - 1), on_plane & (y == ny - 1)
    source = on_x & on_y

    def end1a(i, t):
        return copy(end_in.at[pl.ds(t * pa, pa)], enda, e1s.at[i], e1r.at[0], dev(z, t, y))

    def end1b(i, t):
        return copy(end_in.at[pl.ds(half + t * pb, pb)], endb, e1s.at[nx + i], e1r.at[1], dev(z, x, t))

    def end1():
        return [end1a(i, t) for i, t in enumerate(xs)] + [end1b(i, t) for i, t in enumerate(ys)]

    def end2a(i, t):
        return copy(enda.at[pl.ds(t * qa, qa)], endown.at[pl.ds(0, qa)], e2s.at[i], e2r.at[0], dev(z, x, t))

    def end2b(i, t):
        return copy(endb.at[pl.ds(t * qb, qb)], endown.at[pl.ds(qa, qb)], e2s.at[ny + i], e2r.at[1], dev(z, t, y))

    def end3(i, t):
        at = pl.ds(t * rows, rows)
        return copy(
            endown.at[:, at], zfull.at[pl.ds(qa + qb, qa + qb), at], e3s.at[i], e3r.at[0], dev(t, x, y)
        )

    def each(make, targets):
        return [make(i, t) for i, t in enumerate(targets)]

    def do1():
        wait_recv(tiles_z())
        wait_recv(tiles_y())
        scan = before(tz, z, nz)
        scan_ref[...] = scan
        put_lanes(scan[:, :NH] * factor)

        def scale(q, carry):
            seedc[q] = entry_ref[q] * lanes_ref[q, 0:1]
            return carry

        lax.fori_loop(0, PAIRS, scale, 0)
        start(phase1())
        put_lanes(tile_ref[:, :NH])
        fol_ref[...] = after(ty, y, ny)
        total = tile_ref[...]
        for i in range(ny - 1):
            total = total * ty[i]
        mine_y[...] = total
        start(tiles_x())

        @pl.when(source)
        def _():
            start(end1())

    def do2():
        wait_recv(phase1())
        for q in range(pa):
            total = seedc[x * pa + q]
            for i in range(nx - 1):
                total = total + ra[i, q]
            sa[q] = total
        for q in range(pb):
            total = seedc[half + y * pb + q]
            for i in range(ny - 1):
                total = total + rb[i, q]
            sb[q] = total
        start(phase2())
        wait_recv(tiles_x())
        fol_ref[...] = fol_ref[...] * after(tx, x, nx)
        total = mine_y[...]
        for i in range(nx - 1):
            total = total * tx[i]
        mine_x[...] = total
        start(tiles_p())

        @pl.when(source)
        def _():
            enda[...] = end_in[pl.ds(x * pa, pa)]
            endb[...] = end_in[pl.ds(half + y * pb, pb)]

        @pl.when(on_y)
        def _():
            @pl.when(x != nx - 1)
            def _():
                end1a(0, xs[0]).wait_recv()

            start(each(end2a, ys))
            for q in range(qa):
                endown[q] = enda[y * qa + q]

        @pl.when(on_x)
        def _():
            @pl.when(y != ny - 1)
            def _():
                end1b(0, ys[0]).wait_recv()

            start(each(end2b, xs))
            for q in range(qb):
                endown[qa + q] = endb[x * qb + q]

    def do3():
        wait_recv(phase2())
        for q in range(qa):
            total = sa[y * qa + q]
            for i in range(ny - 1):
                total = total + ra2[i, q]
            own[q] = total
        for q in range(qb):
            total = sb[x * qb + q]
            for i in range(nx - 1):
                total = total + rb2[i, q]
            own[qa + q] = total
        start(phase3())

        @pl.when(on_plane)
        def _():
            @pl.when(y != ny - 1)
            def _():
                end2a(0, ys[0]).wait_recv()

            @pl.when(x != nx - 1)
            def _():
                end2b(0, xs[0]).wait_recv()

            start(each(end3, zs))
            mine = pl.ds(z * rows, rows)
            for q in range(qa + qb):
                zfull[qa + qb + q, mine] = endown[q, mine]

    def do4():
        wait_recv(phase3())
        mine = pl.ds(z * rows, rows)
        for q in range(qa + qb):
            total = own[q, mine]
            for i in range(nz - 1):
                total = total + rz[i, q]
            zfull[q, mine] = total

        @pl.when(jnp.logical_not(on_plane))
        def _():
            end3(0, zs[0]).wait_recv()

        start(phase4())
        wait_recv(tiles_p())
        fol_ref[...] = fol_ref[...] * after(tp, z, nz)

    def do5():
        wait_recv(phase4())
        start(phase5())
        for k, whole in enumerate((seed, end)):
            for q in range(qa):
                whole[la + q] = zfull[k * (qa + qb) + q]
            for q in range(qb):
                whole[lb + q] = zfull[k * (qa + qb) + qa + q]

    def do6():
        wait_recv(phase5())
        start(phase6())

    def do7():
        wait_recv(phase6())

    def drain():
        for phase in (phase1, phase2, phase3, phase4, phase5, phase6, tiles_z, tiles_y, tiles_x, tiles_p):
            wait_send(phase())

        @pl.when(source)
        def _():
            wait_send(end1())

        @pl.when(on_y)
        def _():
            wait_send(each(end2a, ys))

        @pl.when(on_x)
        def _():
            wait_send(each(end2b, xs))

        @pl.when(on_plane)
        def _():
            wait_send(each(end3, zs))

        def finish(q, carry):
            @pl.when(z < nz - 1)
            def _():
                forward(q).wait_send()

            @pl.when(z > 0)
            def _():
                backward(q).wait_send()

            return carry

        lax.fori_loop(0, PAIRS, finish, 0)

    def forward(q):
        return copy(fsend.at[q], pre.at[q], fs.at[q], fr.at[q], dev(lax.rem(z + 1, nz), x, y))

    def backward(q):
        return copy(bsend.at[q], suf.at[q], bs.at[q], br.at[q], dev(lax.rem(z + nz - 1, nz), x, y))

    def step(i):
        cf = i - LAG * z

        @pl.when((cf >= 0) & (cf < PAIRS))
        def _():
            @pl.when(z > 0)
            def _():
                forward(cf).wait_recv()

            @pl.when(z < nz - 1)
            def _():
                fsend[cf] = lanes_ref[cf, 0:1] * pre[cf] + fresh_ref[cf]
                forward(cf).start()

        cb = i - LAG * (nz - 1 - z)

        @pl.when((cb >= 0) & (cb < PAIRS))
        def _():
            @pl.when(z < nz - 1)
            def _():
                backward(cb).wait_recv()

            @pl.when(z > 0)
            def _():
                bsend[cb] = lanes_ref[cb, 0:1] * suf[cb] + entry_ref[cb]
                backward(cb).start()

    def chunk_of(ref, c):
        return ref[:, pl.ds(pl.multiple_of(c * LANES, LANES), LANES)]

    def masked(c):
        return chunk_of(gy_ref, c).astype(F32) * row_mask(len_ref)

    def alone(c):
        spread = spreader(c, NH)
        x_c = chunk_of(rx_ref, c)
        gf = masked(c)
        gy = gf.astype(BF16)
        xf = x_c.astype(F32)
        lane = iota((1, 128), 1) < HD
        q1 = []
        for pair in range(2):
            xp, gp = x_c[:, pair * 128 : pair * 128 + 128], gy[:, pair * 128 : pair * 128 + 128]
            total = [None] * 4
            for odd in range(2):
                j = 2 * pair + odd
                mine = jnp.logical_not(lane) if odd else lane
                xh = jnp.where(mine, xp, jnp.zeros_like(xp))
                gh = jnp.where(mine, gp, jnp.zeros_like(gp))
                col, dcol, arow = a_ch[c, :, j : j + 1], d_ch[c, :, j : j + 1], a_t[c, j : j + 1, :]
                found = [None, None]
                for b in range(4):
                    t0 = (b // 2) * 128
                    sl = slice(b * 64, b * 64 + 64)
                    g = gt[sl, t0:]
                    decay = jnp.exp(jnp.minimum(arow[:, t0:] - col[sl], 0.0))
                    hi, lo = split2(decay * g)
                    gpart = gh[t0:]
                    q = nn(hi, gpart) + nn(lo, gpart)
                    total[b] = q if total[b] is None else total[b] + q
                    k = decay * nt(xh[sl], gpart) * dcol[sl]
                    dgt[sl, t0:] += k
                    part = column(k * g)
                    at = b // 2
                    found[at] = part if found[at] is None else found[at] + part
                row[c, j : j + 1, :] = found[0]
                row[c, j : j + 1, 128:] += found[1]
            q1.append(jnp.concatenate(total, axis=0))
        q1 = jnp.concatenate(q1, axis=1)
        q1_ref[c] = q1
        acc1[...] += by_head(xf * q1, spread)
        outer[...] += by_head(fold8(xf * gf), spread)

    def with_grad(c):
        spread2 = spreader(c, 2 * NH)
        spread = spread2[:NH]
        xf = chunk_of(rx_ref, c).astype(F32)
        gf = masked(c)
        ghi, glo = split2(both(suf, c))
        rb_ = rb_ref[...]
        q2 = nn(rb_, ghi) + nn(rb_, glo)
        wide_w = nn(wcat[...], spread2)
        wide_skip = to_lanes(jnp.broadcast_to(skip_ref[...], (8, NH)), c)[0:1]
        found = factor * (nn(dcat[...], spread2) * q1_ref[c] + wide_w * q2 + wide_skip * gf)
        rdx_ref[:, pl.ds(pl.multiple_of(c * LANES, LANES), LANES)] = found.astype(BF16)
        acc2[...] += by_head(xf * q2, spread)
        whi, wlo = split2(wide_w * xf)
        rdb_ref[...] += nt(whi, ghi) + (nt(wlo, ghi) + nt(whi, glo))

    def with_state(c):
        spread2 = spreader(c, 2 * NH)
        spread = spread2[:NH]
        gf = masked(c)
        state = to_lanes(scan_ref[:, :NH], c)[0:1] * both(end, c) + both(pre, c)
        shi, slo = split2(state)
        rc_ = rc_ref[...]
        cs = nn(rc_, shi) + nn(rc_, slo)
        acc3[...] += by_head(gf * cs, spread)
        ehi, elo = split2(nn(ecat[...], spread2) * gf)
        rdc_ref[...] += nt(ehi, shi) + (nt(elo, shi) + nt(ehi, slo))
        inner[...] += by_head(fold8(state * both(suf, c)), spread)

    def prompt(c):
        spread2 = spreader(c, 2 * NH)
        spread = spread2[:NH]
        pxf = chunk_of(px_ref, c).astype(F32)
        pgrad = to_lanes(fol_ref[:, :NH], c)[1:2] * both(seed, c)
        ghi, glo = split2(pgrad)
        pb_ = pb_ref[...]
        q2 = nn(pb_, ghi) + nn(pb_, glo)
        wide_w = nn(pwcat[...], spread2)
        pdx_ref[:, pl.ds(pl.multiple_of(c * LANES, LANES), LANES)] = (wide_w * q2).astype(BF16)
        pacc[...] += by_head(pxf * q2, spread)
        whi, wlo = split2(wide_w * pxf)
        pdb_ref[...] += nt(whi, ghi) + (nt(wlo, ghi) + nt(whi, glo))
        eye = jnp.where(iota((NS, NS), 0) == iota((NS, NS), 1), 1.0, 0.0).astype(BF16)
        saved = nt(eye, ps_ref[pl.ds(pl.multiple_of(c * LANES, LANES), LANES), :])
        pinner[...] += by_head(fold8(saved * pgrad), spread)

    def closing():
        rate = -jnp.exp(alog)

        def close(zz, d, dstep, da, last):
            cum = exact_nn(upper(), da) + last
            ddt = (dstep + rate * cum) / (1.0 + jnp.exp(-zz))
            return ddt, cum * (rate * d)

        d, rr, e = d_in[...], r_in[...], e_in[...]
        dstep = acc1[...] + rr * acc2[...]
        erow = jnp.concatenate([row[k] for k in range(CHUNKS)], axis=0).T
        da = erow + e * acc3[...] - d * dstep
        last = e[TOK - 1 :] * column(inner[...]) + column(rr * d * acc2[...])
        ddt, dalog = close(z_in[...], d, dstep, da, last)
        ddt = factor * ddt
        rdd_ref[...] = ddt
        bias_sum, alog_sum = column(ddt), factor * column(dalog)
        skip_sum = factor * column(outer[...])

        d, rr = pd[...], pr[...]
        dstep = rr * pacc[...]
        weighted = d * dstep
        last = jnp.exp(column(rate * d)) * column(pinner[...]) + column(weighted)
        ddt, dalog = close(pz[...], d, dstep, -weighted, last)
        pdd_ref[...] = ddt
        terms[...] = jnp.zeros_like(terms)
        terms[0:1, :NH] = bias_sum + column(ddt)
        terms[1:2, :NH] = alog_sum + column(dalog)
        terms[2:3, :NH] = skip_sum

    def scores():
        keep = jnp.where(triangle(), dgt[...], 0.0)
        hi, lo = split2(keep)
        rdb_ref[...] = factor * (rdb_ref[...] + (nn(hi, rc_ref[...]) + nn(lo, rc_ref[...])))
        hi, lo = split2(keep.T)
        rdc_ref[...] = factor * (rdc_ref[...] + (nn(hi, rb_ref[...]) + nn(lo, rb_ref[...])))

    def terms_of(slots, at, send, recv, targets):
        mine = slots.at[at]
        return [copy(mine, mine, send.at[i], recv.at[i], to) for i, to in enumerate(targets)]

    def gather(slots, at, size, send, recv, targets):
        slots[at] = terms[...]
        copies = terms_of(slots, at, send, recv, targets)
        start(copies)
        wait_recv(copies)
        total = slots[0]
        for i in range(1, size):
            total = total + slots[i]
        terms[...] = total
        return copies

    start(tiles_z())
    start(tiles_y())
    prepare()
    first_full = -(-LAG * (nz - 1) // 2)
    turns = first_full + CHUNKS

    def turn(j, carry):
        step(2 * j)

        @pl.when(j < CHUNKS)
        def _():
            alone(j)

        step(2 * j + 1)

        @pl.when(j >= first_full)
        def _():
            with_grad(j - first_full)

        return carry

    done = 0
    for mark, act in zip(MARKS, (do1, do2, do3, do4, do5, do6)):
        lax.fori_loop(done, mark, turn, 0)
        act()
        done = mark
    lax.fori_loop(done, turns, turn, 0)
    do7()

    def rest(c, carry):
        with_state(c)
        prompt(c)
        return carry

    lax.fori_loop(0, CHUNKS, rest, 0)
    closing()
    pending = gather(sx, x, nx, xs_s, xs_r, [dev(z, t, y) for t in xs])
    scores()
    pending += gather(sy, y, ny, ys_s, ys_r, [dev(z, x, t) for t in ys])
    pending += gather(sz, z, nz, zs_s, zs_r, [dev(t, x, y) for t in zs])
    if ndp > 1:
        pending += gather(sd, dp, ndp, ds_s, ds_r, ds)
    small_ref[...] = terms[...]
    wait_send(pending)
    drain()


def factors(count):
    first = 1
    while first * first < count:
        first *= 2
    return first, count // first


def main_call(mesh_shape, *args):
    nz = mesh_shape["ctx"]
    nx, ny = factors(mesh_shape["resp"])
    half = PAIRS // 2
    pa, pb = half // nx, half // ny
    qa, qb = pa // ny, pb // nx
    rows = NS // nz
    vmem = pl.BlockSpec(memory_space=pltpu.VMEM)
    smem = pl.BlockSpec(memory_space=pltpu.SMEM)
    v = lambda *shape: pltpu.VMEM(shape, F32)
    b = lambda *shape: pltpu.VMEM(shape, BF16)
    buf = lambda *lead: pltpu.VMEM(lead + (128,), F32)
    sem = lambda n: pltpu.SemaphoreType.DMA((n,))
    out = jax.ShapeDtypeStruct
    return pl.pallas_call(
        functools.partial(main_kernel, nz, nx, ny),
        out_shape=(
            out((TOK, NH * HD), BF16),
            out((TOK, NS), F32),
            out((TOK, NH), F32),
            out((TOK, NH * HD), BF16),
            out((TOK, NS), F32),
            out((TOK, NS), F32),
            out((TOK, NH), F32),
            out((8, 128), F32),
        ),
        in_specs=[smem] * 2 + [vmem] * 16,
        out_specs=(vmem,) * 8,
        scratch_shapes=[
            v(CHUNKS, TOK, PER), v(CHUNKS, TOK, PER), v(CHUNKS, PER, TOK), v(TOK, TOK), v(TOK, TOK),
            v(CHUNKS, TOK, LANES), b(TOK, 2 * NH), b(TOK, 2 * NH), b(TOK, 2 * NH),
            v(TOK, NH), v(TOK, NH), v(TOK, NH), v(TOK, NH), v(CHUNKS, PER, TOK),
            v(TOK, NH), v(TOK, NH), v(TOK, NH), v(8, NH), v(8, NH),
            b(TOK, 2 * NH), v(TOK, NH), v(TOK, NH), v(TOK, NH), v(TOK, NH), v(8, NH), buf(8), buf(8), buf(PAIRS, 8),
        ]
        + [buf(PAIRS, NS)] * 7
        + [
            buf(nx - 1, pa, NS), buf(ny - 1, pb, NS), buf(pa, NS), buf(pb, NS), buf(ny - 1, qa, NS),
            buf(nx - 1, qb, NS), buf(qa + qb, NS), buf(nz - 1, qa + qb, rows), buf(2 * (qa + qb), NS),
            buf(pa, NS), buf(pb, NS), buf(qa + qb, NS),
            buf(nz, 8), buf(ny, 8), buf(nx, 8), buf(nz, 8), buf(8), buf(8),
            buf(nx, 8), buf(ny, 8), buf(nz, 8), buf(2, 8), buf(8),
        ]
        + [sem(PAIRS)] * 4
        + [sem(nx + ny)] * 4
        + [sem(nz)] * 4
        + [sem(2 * (nx + ny))] * 4
        + [sem(nx + ny), sem(2), sem(nx + ny), sem(2), sem(nz), sem(1)]
        + [sem(nz)] * 2 + [sem(ny)] * 2 + [sem(nx)] * 2 + [sem(nz)] * 2
        + [sem(nx)] * 2 + [sem(ny)] * 2 + [sem(nz)] * 2 + [sem(2)] * 2,
        compiler_params=pltpu.CompilerParams(collective_id=0, has_side_effects=True, vmem_limit_bytes=LIMIT),
        name="main",
    )(*args)


def body(
    mesh_shape,
    prompt_x, prompt_b, prompt_dt, prompt_states, resp_x, resp_b, resp_c, resp_dt, grad_out, lengths, advantages,
    dt_bias, a_log, skip,
):
    nz = mesh_shape["ctx"]
    px, pb, pdt = prompt_x[0], prompt_b[0], prompt_dt[0]
    ps = prompt_states.reshape(NH * HD, NS)
    rx, rb, rc, rdt, gy = resp_x[0, 0], resp_b[0, 0], resp_c[0, 0], resp_dt[0, 0], grad_out[0, 0]
    bias, alog = dt_bias[None], a_log[None]
    factor = advantages * float(nz * TOK) / lengths.astype(F32)
    fresh, entry, end, tile = first_call(lengths, rx, rb, rc, rdt, gy, px, pb, pdt, ps, bias, alog)
    pdx, pdb, pdd, rdx, rdb, rdc, rdd, small = main_call(
        mesh_shape, lengths, factor, fresh, entry, end, tile,
        rx, rb, rc, rdt, gy, px, pb, pdt, ps, bias, alog, skip[None],
    )
    return (
        pdx[None], pdb[None], pdd[None], rdx[None, None], rdb[None, None], rdc[None, None], rdd[None, None],
        small[0, :NH], small[1, :NH], small[2, :NH],
    )


def solution(mesh):
    wide = P("dp", ("ctx", "resp"), None)
    long = P("dp", "resp", "ctx", None)
    in_specs = (
        wide, wide, wide, P("dp", ("ctx", "resp"), None, None, None), long, long, long, long, long,
        P("dp", "resp"), P("dp", "resp"), P(), P(), P(),
    )
    out_specs = (wide, wide, wide, long, long, long, long, P(), P(), P())
    return jax.shard_map(
        functools.partial(body, dict(mesh.shape)), mesh=mesh, in_specs=in_specs, out_specs=out_specs, check_vma=False
    )
```

time: 629 us -> 188 us (0.30)
  blocking collectives: 447 us -> 0 us
    all_gather x1 -> x0, blocking collectives: 294 us -> none  [body(): every = lax.all_gather(decays, ('ctx', 'resp'))]
    psum x1 -> x0, blocking collectives: 153 us -> none  [body(): small = lax.psum(small, ('dp', 'ctx', 'resp'))]
    unnamed x8 -> x17, local copies, waits for them, and re-layouts: 5.15 us -> 13 us
    pallas_call x2 -> x1, Pallas kernels: 151 us -> 155 us  [main_call(): pl.pallas_call(functools.partial(main_kernel, nz, nx, ny), out_shape=(out...]
where the time goes in v2:
time: 188 us; the launch traced here: 187 us
  Pallas kernels  171 us (91%)
  local copies, waits for them, and re-layouts  14.3 us (8%)
  between operations  2 us (1%)
    pallas_call x1, Pallas kernels, main_call(): pl.pallas_call(functools.partial(main_kernel, nz, nx, ny), out_shape=(out...  155 us
    pallas_call x1, Pallas kernels, first_call(): pl.pallas_call(first_kernel, grid=(CHUNKS,), out_shape=(shape, shape, sha...  15.4 us
    unnamed x17, local copies, waits for them, and re-layouts  13 us

profile of v2, /device:TPU:1, one launch (start us, length us, event | category | flops | bytes accessed | tf_op | source)
XLA Modules:
  0.0 186.9 jit_solution(10905620140831618104)
XLA Ops:
  2.0 1.6 copy.25
  3.6 1.6 copy.24
  5.2 15.4 %first.1 = (f32[32,128,128]{2,1,0:T(8,128)}, f32[32,128,128]{2,1,0:T(8,128)}, f32[32,128,128]{2,1,0:T(8,128)}, f32[8,128]{1,0:T(8,128)}) custom-call(s32[1,1]{1,0:T(1,128)S(6)} %copy.33.len_ref, bf16[256,4096]{1,0:T(8,128)(2,1)} %bitcast.25, bf16[256,128]{1,0:T(8,128)(2,1)} %bitcast.39, bf16[256,128]{1,0:T(8,128)(2,1)} %bitcast.41, f32[256,64]{1,0:T(8,128)} %bitcast.37, ...), custom_call_target="tpu_custom_call" | custom-call | tf_op jit(solution)/shard_map/first/pallas_call | solution.py:172
  20.6 155.2 %main.1 = (bf16[256,4096]{1,0:T(8,128)(2,1)}, f32[256,128]{1,0:T(8,128)}, f32[256,64]{1,0:T(8,128)}, bf16[256,4096]{1,0:T(8,128)(2,1)}, f32[256,128]{1,0:T(8,128...) custom-call(s32[1,1]{1,0:T(1,128)S(6)} %copy.33.len_ref, f32[1,1]{1,0:T(1,128)S(6)} %div.3.fac_ref, ...), custom_call_target="tpu_custom_call" | custom-call | tf_op jit(solution)/shard_map/main/pallas_call | solution.py:832
  175.8 1.3 slice_bitcast_fusion
  177.1 1.6 copy.26
  178.7 1.6 copy.27
  180.3 0.0 copy-start.3
  180.3 0.0 copy-start
  180.3 3.3 %copy.35 = bf16[1,256,4096]{2,1,0:T(8,128)(2,1)} copy(bf16[1,256,4096]{2,1,0:T(8,128)(2,1)} %bitcast.34) | data formatting | bytes 4194304
  183.6 0.0 copy-done.3
  183.6 0.7 copy.36
  184.3 0.0 copy-done
  184.3 0.0 copy-start.2
  184.3 0.0 copy-start.1
  184.3 1.3 copy.37
  185.6 0.0 copy-done.2
  185.6 0.7 copy.38
  186.2 0.0 copy-done.1
  186.2 0.7 copy.39
Async XLA Ops:
  180.3 3.3 %copy-start.3 = (f32[256,128]{1,0:T(8,128)S(1)}, f32[256,128]{1,0:T(8,128)}, u32[]{:S(2)}) copy-start(f32[256,128]{1,0:T(8,128)} %get-tuple-element.27) | copy-start | bytes 393220
  180.3 3.9 %copy-start = (bf16[256,4096]{1,0:T(8,128)(2,1)S(1)}, bf16[256,4096]{1,0:T(8,128)(2,1)}, u32[]{:S(2)}) copy-start(bf16[256,4096]{1,0:T(8,128)(2,1)} %get-tuple-element.29) | copy-start | bytes 6291460
  184.3 1.3 copy-start.2
  184.3 2.0 %copy-start.1 = (f32[256,128]{1,0:T(8,128)S(1)}, f32[256,128]{1,0:T(8,128)}, u32[]{:S(2)}) copy-start(f32[256,128]{1,0:T(8,128)} %get-tuple-element.31) | copy-start | bytes 393220

commit v3 on v2

--- a/solution.py
+++ b/solution.py
@@ -110,109 +110,18 @@
     return jnp.where(position < length_ref[0, 0], 1.0, 0.0)
 
 
-def first_kernel(
-    len_ref, rx_ref, rb_ref, rc_ref, rdt_ref, gy_ref, px_ref, pb_ref, pdt_ref, ps_ref, bias_ref, alog_ref,
-    fresh_ref, entry_ref, end_ref, decay_ref,
-    wcat, ecat, bt, ct, pwcat, pecat, pbt,
-):
-    c = pl.program_id(0)
-    last = (lax.axis_index("ctx") == lax.axis_size("ctx") - 1) & (
-        lax.axis_index("resp") == lax.axis_size("resp") - 1
-    )
-
-    @pl.when(c == 0)
-    def _():
-        bias, alog = bias_ref[...], alog_ref[...]
-        _, d, _, a = steps(rdt_ref[...], bias, alog)
-        wcat[...] = cat2(jnp.exp(a[TOK - 1 :, :] - a) * d)
-        ecat[...] = cat2(jnp.exp(a) * row_mask(len_ref))
-        bt[...] = rb_ref[...].astype(F32).T.astype(BF16)
-        ct[...] = rc_ref[...].astype(F32).T.astype(BF16)
-        decay_ref[...] = jnp.ones_like(decay_ref)
-        decay_ref[0:1, :NH] = jnp.exp(a[TOK - 1 :, :])
-        _, _, _, a = steps(pdt_ref[...], bias, alog)
-        decay_ref[1:2, :NH] = jnp.exp(a[TOK - 1 :, :])
-
-    @pl.when((c == 0) & last)
-    def _():
-        bias, alog = bias_ref[...], alog_ref[...]
-        _, d, _, a = steps(pdt_ref[...], bias, alog)
-        pwcat[...] = cat2(jnp.exp(a[TOK - 1 :, :] - a) * d)
-        pecat[...] = cat2(jnp.broadcast_to(jnp.exp(a[TOK - 1 :, :]), (NS, NH)))
-        pbt[...] = pb_ref[...].astype(F32).T.astype(BF16)
-
-    spread = spreader(c, 2 * NH)
-
-    def put(ref, value):
-        ref[0] = value[:, :128]
-        ref[1] = value[:, 128:]
-
-    hi, lo = split2(nn(wcat[...], spread) * rx_ref[...].astype(F32))
-    put(fresh_ref, nn(bt[...], hi) + nn(bt[...], lo))
-    hi, lo = split2(nn(ecat[...], spread) * gy_ref[...].astype(F32))
-    put(entry_ref, nn(ct[...], hi) + nn(ct[...], lo))
-
-    @pl.when(last)
-    def _():
-        hi, lo = split2(nn(pwcat[...], spread) * px_ref[...].astype(F32))
-        eye = jnp.where(iota((NS, NS), 0) == iota((NS, NS), 1), 1.0, 0.0).astype(BF16)
-        saved = nt(eye, ps_ref[...])
-        put(end_ref, nn(pecat[...], spread) * saved + (nn(pbt[...], hi) + nn(pbt[...], lo)))
-
-    @pl.when(jnp.logical_not(last))
-    def _():
-        end_ref[...] = jnp.zeros_like(end_ref)
-
-
-def first_call(length, rx, rb, rc, rdt, gy, px, pb, pdt, ps, bias, alog):
-    wide = pl.BlockSpec((TOK, LANES), lambda c: (0, c))
-    whole = lambda shape: pl.BlockSpec(shape, lambda c: (0,) * len(shape))
-    state = pl.BlockSpec((2, NS, 128), lambda c: (c, 0, 0))
-    shape = jax.ShapeDtypeStruct((PAIRS, NS, 128), F32)
-    return pl.pallas_call(
-        first_kernel,
-        grid=(CHUNKS,),
-        out_shape=(shape, shape, shape, jax.ShapeDtypeStruct((8, 128), F32)),
-        in_specs=[
-            pl.BlockSpec(memory_space=pltpu.SMEM),
-            wide,
-            whole((TOK, NS)),
-            whole((TOK, NS)),
-            whole((TOK, NH)),
-            wide,
-            wide,
-            whole((TOK, NS)),
-            whole((TOK, NH)),
-            pl.BlockSpec((LANES, NS), lambda c: (c, 0)),
-            whole((1, NH)),
-            whole((1, NH)),
-        ],
-        out_specs=(state, state, state, whole((8, 128))),
-        scratch_shapes=[
-            pltpu.VMEM((TOK, 2 * NH), BF16),
-            pltpu.VMEM((TOK, 2 * NH), BF16),
-            pltpu.VMEM((NS, TOK), BF16),
-            pltpu.VMEM((NS, TOK), BF16),
-            pltpu.VMEM((TOK, 2 * NH), BF16),
-            pltpu.VMEM((NS, 2 * NH), BF16),
-            pltpu.VMEM((NS, TOK), BF16),
-        ],
-        compiler_params=pltpu.CompilerParams(vmem_limit_bytes=LIMIT),
-        name="first",
-    )(length, rx, rb, rc, rdt, gy, px, pb, pdt, ps, bias, alog)
-
-
 LAG = 3
-MARKS = (1, 6, 8, 10, 13, 16)
+MARKS = (5, 7, 8, 9, 10, 11, 12, 13)
 
 
 def main_kernel(
     nz, nx, ny,
-    len_ref, fac_ref, fresh_ref, entry_ref, end_in, tile_ref,
+    len_ref, fac_ref,
     rx_ref, rb_ref, rc_ref, rdt_ref, gy_ref, px_ref, pb_ref, pdt_ref, ps_ref, bias_ref, alog_ref, skip_ref,
     pdx_ref, pdb_ref, pdd_ref, rdx_ref, rdb_ref, rdc_ref, rdd_ref, small_ref,
     a_ch, d_ch, a_t, gt, dgt, q1_ref, dcat, wcat, ecat, e_in, r_in, d_in, z_in, row, acc1, acc2, acc3, inner, outer,
     pwcat, pr, pd, pz, pacc, pinner, scan_ref, fol_ref, lanes_ref,
+    bt, ct, pbt, pecat, tile_ref, fresh_ref, entry_ref, end_in,
     pre, suf, fsend, bsend, seedc, seed, end, ra, rb, sa, sb, ra2, rb2, own, rz, zfull, enda, endb, endown,
     tz, ty, tx, tp, mine_y, mine_x, sx, sy, sz, sd, terms,
     fs, fr, bs, br, s1, r1, s2, r2, s3, r3, s4, r4, s5, r5, s6, r6, e1s, e1r, e2s, e2r, e3s, e3r,
@@ -240,7 +149,7 @@
     bias, alog = bias_ref[...], alog_ref[...]
 
     def prepare():
-        zz, d, _, a = steps(rdt_ref[...], bias, alog)
+        zz, d, _, a = steps(rdt_ref[...].T, bias, alog)
         z_in[...] = zz
         d_in[...] = d
         at = a.T
@@ -255,40 +164,73 @@
         dcat[...] = cat2(d)
         wcat[...] = cat2(rr * d)
         ecat[...] = cat2(e)
+        tile_ref[...] = jnp.ones_like(tile_ref)
+        tile_ref[0:1, :NH] = e[TOK - 1 :]
+        zz, d, _, a = steps(pdt_ref[...].T, bias, alog)
+        pz[...] = zz
+        pd[...] = d
+        rr = jnp.exp(a[TOK - 1 :, :] - a)
+        pr[...] = rr
+        pwcat[...] = cat2(rr * d)
+        tile_ref[1:2, :NH] = jnp.exp(a[TOK - 1 :, :])
+        bt[...] = rb_ref[...].astype(F32).T.astype(BF16)
+        ct[...] = rc_ref[...].astype(F32).T.astype(BF16)
+
+    def prepare_rest():
         scores = nt(rb_ref[...], rc_ref[...])
         gt[...] = jnp.where(triangle(), scores, 0.0)
         dgt[...] = jnp.zeros_like(dgt)
         for acc in (acc1, acc2, acc3, inner, outer, pacc, pinner, rdb_ref, rdc_ref, pdb_ref):
             acc[...] = jnp.zeros_like(acc)
-        zz, d, _, a = steps(pdt_ref[...], bias, alog)
-        pz[...] = zz
-        pd[...] = d
-        rr = jnp.exp(a[TOK - 1 :, :] - a)
-        pr[...] = rr
-        pwcat[...] = cat2(rr * d)
+        for c in range(CHUNKS):
+            put(lanes_ref, c, to_lanes(tile_ref[:, :NH], c))
+
+        @pl.when(z == 0)
+        def _():
+            pre[...] = jnp.zeros_like(pre)
+
+        @pl.when(z == nz - 1)
+        def _():
+            suf[...] = jnp.zeros_like(suf)
 
     def to_lanes(v, c):
         return nn(cat3(v), spreader(c, 3 * NH))
 
-    def put_lanes(v):
+    def put(ref, c, value):
+        ref[2 * c] = value[:, :128]
+        ref[2 * c + 1] = value[:, 128:]
+
+    def chunk_of(ref, c):
+        return ref[:, pl.ds(pl.multiple_of(c * LANES, LANES), LANES)]
+
+    def masked(c):
+        return chunk_of(gy_ref, c).astype(F32) * row_mask(len_ref)
+
+    def add_entry(c):
+        hi, lo = split2(nn(ecat[...], spreader(c, 2 * NH)) * masked(c))
+        put(entry_ref, c, nn(ct[...], hi) + nn(ct[...], lo))
+
+    def add_fresh(c):
+        hi, lo = split2(nn(wcat[...], spreader(c, 2 * NH)) * chunk_of(rx_ref, c).astype(F32))
+        put(fresh_ref, c, nn(bt[...], hi) + nn(bt[...], lo))
+
+    def saved_state(c):
+        eye = jnp.where(iota((NS, NS), 0) == iota((NS, NS), 1), 1.0, 0.0).astype(BF16)
+        return nt(eye, ps_ref[pl.ds(pl.multiple_of(c * LANES, LANES), LANES), :])
+
+    def last_state():
+        pbt[...] = pb_ref[...].astype(F32).T.astype(BF16)
+        pecat[...] = cat2(jnp.broadcast_to(tile_ref[1:2, :NH], (NS, NH)))
+
         def one(c, carry):
-            wide = to_lanes(v, c)
-            lanes_ref[2 * c] = wide[:, :128]
-            lanes_ref[2 * c + 1] = wide[:, 128:]
+            spread = spreader(c, 2 * NH)
+            hi, lo = split2(nn(pwcat[...], spread) * chunk_of(px_ref, c).astype(F32))
+            put(end_in, c, nn(pecat[...], spread) * saved_state(c) + (nn(pbt[...], hi) + nn(pbt[...], lo)))
             return carry
 
-        lax.fori_loop(0, CHUNKS, one, 0)
-
-    put_lanes(tile_ref[:, :NH])
-
-    @pl.when(z == 0)
-    def _():
-        pre[...] = jnp.zeros_like(pre)
-
-    @pl.when(z == nz - 1)
-    def _():
-        suf[...] = jnp.zeros_like(suf)
-
+        lax.fori_loop(0, CHUNKS, one, 0, unroll=2)
+
+    prepare()
     pl.semaphore_wait(barrier, len(partners))
 
     def copy(src, dst, send, recv, to):
@@ -356,38 +298,30 @@
             for i, t in enumerate(zs)
         ]
 
-    def phase4():
-        mine = zfull.at[:, pl.ds(z * rows, rows)]
-        return [copy(mine, mine, s4.at[i], r4.at[i], dev(t, x, y)) for i, t in enumerate(zs)]
+    def phase4(k):
+        mine = zfull.at[pl.ds(k * (qa + qb), qa + qb), pl.ds(z * rows, rows)]
+        return [copy(mine, mine, s4.at[k * nz + i], r4.at[k * nz + i], dev(t, x, y)) for i, t in enumerate(zs)]
 
     la, lb = x * pa + y * qa, half + y * pb + x * qb
 
-    def phase5():
-        found = []
-        for k, whole in enumerate((seed, end)):
-            for i, t in enumerate(ys):
-                at = k * (nx + ny) + i
-                found.append(
-                    copy(zfull.at[pl.ds(k * (qa + qb), qa)], whole.at[pl.ds(la, qa)], s5.at[at], r5.at[at], dev(z, x, t))
-                )
-            for i, t in enumerate(xs):
-                at = k * (nx + ny) + ny + i
-                found.append(
-                    copy(zfull.at[pl.ds(k * (qa + qb) + qa, qb)], whole.at[pl.ds(lb, qb)], s5.at[at], r5.at[at], dev(z, t, y))
-                )
+    def phase5(k):
+        whole, found = (seed, end)[k], []
+        for i, t in enumerate(ys):
+            at, src = k * (nx + ny) + i, zfull.at[pl.ds(k * (qa + qb), qa)]
+            found.append(copy(src, whole.at[pl.ds(la, qa)], s5.at[at], r5.at[at], dev(z, x, t)))
+        for i, t in enumerate(xs):
+            at, src = k * (nx + ny) + ny + i, zfull.at[pl.ds(k * (qa + qb) + qa, qb)]
+            found.append(copy(src, whole.at[pl.ds(lb, qb)], s5.at[at], r5.at[at], dev(z, t, y)))
         return found
 
-    def phase6():
-        found = []
-        for k, whole in enumerate((end, seed)):
-            for i, t in enumerate(xs):
-                at = k * (nx + ny) + i
-                mine = whole.at[pl.ds(x * pa, pa)]
-                found.append(copy(mine, mine, s6.at[at], r6.at[at], dev(z, t, y)))
-            for i, t in enumerate(ys):
-                at = k * (nx + ny) + nx + i
-                mine = whole.at[pl.ds(half + y * pb, pb)]
-                found.append(copy(mine, mine, s6.at[at], r6.at[at], dev(z, x, t)))
+    def phase6(k):
+        whole, found = (seed, end)[k], []
+        for i, t in enumerate(xs):
+            at, mine = k * (nx + ny) + i, whole.at[pl.ds(x * pa, pa)]
+            found.append(copy(mine, mine, s6.at[at], r6.at[at], dev(z, t, y)))
+        for i, t in enumerate(ys):
+            at, mine = k * (nx + ny) + nx + i, whole.at[pl.ds(half + y * pb, pb)]
+            found.append(copy(mine, mine, s6.at[at], r6.at[at], dev(z, x, t)))
         return found
 
     on_plane = z == nz - 1
@@ -420,18 +354,14 @@
 
     def do1():
         wait_recv(tiles_z())
-        wait_recv(tiles_y())
         scan = before(tz, z, nz)
         scan_ref[...] = scan
-        put_lanes(scan[:, :NH] * factor)
-
-        def scale(q, carry):
-            seedc[q] = entry_ref[q] * lanes_ref[q, 0:1]
-            return carry
-
-        lax.fori_loop(0, PAIRS, scale, 0)
+        for c in range(CHUNKS):
+            wide = to_lanes(scan[:, :NH] * factor, c)
+            seedc[2 * c] = entry_ref[2 * c] * wide[0:1, :128]
+            seedc[2 * c + 1] = entry_ref[2 * c + 1] * wide[0:1, 128:]
         start(phase1())
-        put_lanes(tile_ref[:, :NH])
+        wait_recv(tiles_y())
         fol_ref[...] = after(ty, y, ny)
         total = tile_ref[...]
         for i in range(ny - 1):
@@ -441,6 +371,7 @@
 
         @pl.when(source)
         def _():
+            last_state()
             start(end1())
 
     def do2():
@@ -464,6 +395,7 @@
         mine_x[...] = total
         start(tiles_p())
 
+    def end_2():
         @pl.when(source)
         def _():
             enda[...] = end_in[pl.ds(x * pa, pa)]
@@ -491,6 +423,7 @@
 
     def do3():
         wait_recv(phase2())
+        wait_send(phase1())
         for q in range(qa):
             total = sa[y * qa + q]
             for i in range(ny - 1):
@@ -503,6 +436,7 @@
             own[qa + q] = total
         start(phase3())
 
+    def end_3():
         @pl.when(on_plane)
         def _():
             @pl.when(y != ny - 1)
@@ -526,34 +460,36 @@
             for i in range(nz - 1):
                 total = total + rz[i, q]
             zfull[q, mine] = total
-
-        @pl.when(jnp.logical_not(on_plane))
-        def _():
-            end3(0, zs[0]).wait_recv()
-
-        start(phase4())
+        start(phase4(0))
         wait_recv(tiles_p())
         fol_ref[...] = fol_ref[...] * after(tp, z, nz)
 
-    def do5():
-        wait_recv(phase4())
-        start(phase5())
-        for k, whole in enumerate((seed, end)):
-            for q in range(qa):
-                whole[la + q] = zfull[k * (qa + qb) + q]
-            for q in range(qb):
-                whole[lb + q] = zfull[k * (qa + qb) + qa + q]
-
-    def do6():
-        wait_recv(phase5())
-        start(phase6())
-
-    def do7():
-        wait_recv(phase6())
+    def end_4():
+        @pl.when(jnp.logical_not(on_plane))
+        def _():
+            end3(0, zs[0]).wait_recv()
+
+        start(phase4(1))
+
+    def spread_5(k):
+        whole = (seed, end)[k]
+        wait_recv(phase4(k))
+        start(phase5(k))
+        for q in range(qa):
+            whole[la + q] = zfull[k * (qa + qb) + q]
+        for q in range(qb):
+            whole[lb + q] = zfull[k * (qa + qb) + qa + q]
+
+    def spread_6(k):
+        wait_recv(phase5(k))
+        start(phase6(k))
 
     def drain():
-        for phase in (phase1, phase2, phase3, phase4, phase5, phase6, tiles_z, tiles_y, tiles_x, tiles_p):
+        for phase in (phase2, phase3, tiles_z, tiles_y, tiles_x, tiles_p):
             wait_send(phase())
+        for phase in (phase4, phase5, phase6):
+            wait_send(phase(0))
+            wait_send(phase(1))
 
         @pl.when(source)
         def _():
@@ -616,12 +552,6 @@
             def _():
                 bsend[cb] = lanes_ref[cb, 0:1] * suf[cb] + entry_ref[cb]
                 backward(cb).start()
-
-    def chunk_of(ref, c):
-        return ref[:, pl.ds(pl.multiple_of(c * LANES, LANES), LANES)]
-
-    def masked(c):
-        return chunk_of(gy_ref, c).astype(F32) * row_mask(len_ref)
 
     def alone(c):
         spread = spreader(c, NH)
@@ -693,30 +623,33 @@
         inner[...] += by_head(fold8(state * both(suf, c)), spread)
 
     def prompt(c):
-        spread2 = spreader(c, 2 * NH)
-        spread = spread2[:NH]
+        spread = spreader(c, NH)
         pxf = chunk_of(px_ref, c).astype(F32)
         pgrad = to_lanes(fol_ref[:, :NH], c)[1:2] * both(seed, c)
+        put(seedc, c, pgrad)
         ghi, glo = split2(pgrad)
         pb_ = pb_ref[...]
         q2 = nn(pb_, ghi) + nn(pb_, glo)
-        wide_w = nn(pwcat[...], spread2)
-        pdx_ref[:, pl.ds(pl.multiple_of(c * LANES, LANES), LANES)] = (wide_w * q2).astype(BF16)
+        q1_ref[c] = q2
         pacc[...] += by_head(pxf * q2, spread)
+        pinner[...] += by_head(fold8(saved_state(c) * pgrad), spread)
+
+    def prompt_rest(c):
+        pxf = chunk_of(px_ref, c).astype(F32)
+        ghi, glo = split2(both(seedc, c))
+        wide_w = nn(pwcat[...], spreader(c, 2 * NH))
+        pdx_ref[:, pl.ds(pl.multiple_of(c * LANES, LANES), LANES)] = (wide_w * q1_ref[c]).astype(BF16)
         whi, wlo = split2(wide_w * pxf)
         pdb_ref[...] += nt(whi, ghi) + (nt(wlo, ghi) + nt(whi, glo))
-        eye = jnp.where(iota((NS, NS), 0) == iota((NS, NS), 1), 1.0, 0.0).astype(BF16)
-        saved = nt(eye, ps_ref[pl.ds(pl.multiple_of(c * LANES, LANES), LANES), :])
-        pinner[...] += by_head(fold8(saved * pgrad), spread)
-
-    def closing():
-        rate = -jnp.exp(alog)
-
-        def close(zz, d, dstep, da, last):
-            cum = exact_nn(upper(), da) + last
-            ddt = (dstep + rate * cum) / (1.0 + jnp.exp(-zz))
-            return ddt, cum * (rate * d)
-
+
+    rate = -jnp.exp(alog)
+
+    def close(zz, d, dstep, da, last):
+        cum = exact_nn(upper(), da) + last
+        ddt = (dstep + rate * cum) / (1.0 + jnp.exp(-zz))
+        return ddt, cum * (rate * d)
+
+    def close_resp():
         d, rr, e = d_in[...], r_in[...], e_in[...]
         dstep = acc1[...] + rr * acc2[...]
         erow = jnp.concatenate([row[k] for k in range(CHUNKS)], axis=0).T
@@ -724,20 +657,21 @@
         last = e[TOK - 1 :] * column(inner[...]) + column(rr * d * acc2[...])
         ddt, dalog = close(z_in[...], d, dstep, da, last)
         ddt = factor * ddt
-        rdd_ref[...] = ddt
-        bias_sum, alog_sum = column(ddt), factor * column(dalog)
-        skip_sum = factor * column(outer[...])
-
+        rdd_ref[...] = ddt.T
+        terms[...] = jnp.zeros_like(terms)
+        terms[0:1, :NH] = column(ddt)
+        terms[1:2, :NH] = factor * column(dalog)
+        terms[2:3, :NH] = factor * column(outer[...])
+
+    def close_prompt():
         d, rr = pd[...], pr[...]
         dstep = rr * pacc[...]
         weighted = d * dstep
         last = jnp.exp(column(rate * d)) * column(pinner[...]) + column(weighted)
         ddt, dalog = close(pz[...], d, dstep, -weighted, last)
-        pdd_ref[...] = ddt
-        terms[...] = jnp.zeros_like(terms)
-        terms[0:1, :NH] = bias_sum + column(ddt)
-        terms[1:2, :NH] = alog_sum + column(dalog)
-        terms[2:3, :NH] = skip_sum
+        pdd_ref[...] = ddt.T
+        terms[0:1, :NH] += column(ddt)
+        terms[1:2, :NH] += column(dalog)
 
     def scores():
         keep = jnp.where(triangle(), dgt[...], 0.0)
@@ -750,10 +684,11 @@
         mine = slots.at[at]
         return [copy(mine, mine, send.at[i], recv.at[i], to) for i, to in enumerate(targets)]
 
-    def gather(slots, at, size, send, recv, targets):
+    def gather(slots, at, size, send, recv, targets, beside):
         slots[at] = terms[...]
         copies = terms_of(slots, at, send, recv, targets)
         start(copies)
+        beside()
         wait_recv(copies)
         total = slots[0]
         for i in range(1, size):
@@ -763,11 +698,25 @@
 
     start(tiles_z())
     start(tiles_y())
-    prepare()
+
+    def looped(work, lo, hi, unroll=2):
+        def one(c, carry):
+            work(c)
+            return carry
+
+        lax.fori_loop(lo, hi, one, 0, unroll=unroll)
+
+    looped(add_entry, 0, CHUNKS)
+    do1()
+    prepare_rest()
     first_full = -(-LAG * (nz - 1) // 2)
     turns = first_full + CHUNKS
 
     def turn(j, carry):
+        @pl.when(j < CHUNKS)
+        def _():
+            add_fresh(j)
+
         step(2 * j)
 
         @pl.when(j < CHUNKS)
@@ -783,26 +732,30 @@
         return carry
 
     done = 0
-    for mark, act in zip(MARKS, (do1, do2, do3, do4, do5, do6)):
+    acts = (
+        lambda: (do2(), end_2()), lambda: (do3(), end_3()), end_4, do4,
+        lambda: spread_5(1), lambda: spread_5(0), lambda: spread_6(1), lambda: spread_6(0),
+    )
+    for mark, act in zip(MARKS, acts):
         lax.fori_loop(done, mark, turn, 0)
         act()
         done = mark
     lax.fori_loop(done, turns, turn, 0)
-    do7()
-
-    def rest(c, carry):
-        with_state(c)
-        prompt(c)
-        return carry
-
-    lax.fori_loop(0, CHUNKS, rest, 0)
-    closing()
-    pending = gather(sx, x, nx, xs_s, xs_r, [dev(z, t, y) for t in xs])
-    scores()
-    pending += gather(sy, y, ny, ys_s, ys_r, [dev(z, x, t) for t in ys])
-    pending += gather(sz, z, nz, zs_s, zs_r, [dev(t, x, y) for t in zs])
-    if ndp > 1:
-        pending += gather(sd, dp, ndp, ds_s, ds_r, ds)
+    wait_recv(phase6(1))
+    looped(with_state, 0, CHUNKS)
+    close_resp()
+    wait_recv(phase6(0))
+    looped(prompt, 0, CHUNKS)
+    close_prompt()
+    part = CHUNKS // 4
+    pending = gather(sx, x, nx, xs_s, xs_r, [dev(z, t, y) for t in xs], lambda: looped(prompt_rest, 0, part))
+    pending += gather(
+        sy, y, ny, ys_s, ys_r, [dev(z, x, t) for t in ys], lambda: looped(prompt_rest, part, 2 * part)
+    )
+    pending += gather(
+        sz, z, nz, zs_s, zs_r, [dev(t, x, y) for t in zs], lambda: looped(prompt_rest, 2 * part, CHUNKS)
+    )
+    pending += gather(sd, dp, ndp, ds_s, ds_r, ds, scores)
     small_ref[...] = terms[...]
     wait_send(pending)
     drain()
@@ -834,14 +787,14 @@
         out_shape=(
             out((TOK, NH * HD), BF16),
             out((TOK, NS), F32),
-            out((TOK, NH), F32),
+            out((NH, TOK), F32),
             out((TOK, NH * HD), BF16),
             out((TOK, NS), F32),
             out((TOK, NS), F32),
-            out((TOK, NH), F32),
+            out((NH, TOK), F32),
             out((8, 128), F32),
         ),
-        in_specs=[smem] * 2 + [vmem] * 16,
+        in_specs=[smem] * 2 + [vmem] * 12,
         out_specs=(vmem,) * 8,
         scratch_shapes=[
             v(CHUNKS, TOK, PER), v(CHUNKS, TOK, PER), v(CHUNKS, PER, TOK), v(TOK, TOK), v(TOK, TOK),
@@ -849,8 +802,9 @@
             v(TOK, NH), v(TOK, NH), v(TOK, NH), v(TOK, NH), v(CHUNKS, PER, TOK),
             v(TOK, NH), v(TOK, NH), v(TOK, NH), v(8, NH), v(8, NH),
             b(TOK, 2 * NH), v(TOK, NH), v(TOK, NH), v(TOK, NH), v(TOK, NH), v(8, NH), buf(8), buf(8), buf(PAIRS, 8),
+            b(NS, TOK), b(NS, TOK), b(NS, TOK), b(NS, 2 * NH), buf(8),
         ]
-        + [buf(PAIRS, NS)] * 7
+        + [buf(PAIRS, NS)] * 10
         + [
             buf(nx - 1, pa, NS), buf(ny - 1, pb, NS), buf(pa, NS), buf(pb, NS), buf(ny - 1, qa, NS),
             buf(nx - 1, qb, NS), buf(qa + qb, NS), buf(nz - 1, qa + qb, rows), buf(2 * (qa + qb), NS),
@@ -860,7 +814,8 @@
         ]
         + [sem(PAIRS)] * 4
         + [sem(nx + ny)] * 4
-        + [sem(nz)] * 4
+        + [sem(nz)] * 2
+        + [sem(2 * nz)] * 2
         + [sem(2 * (nx + ny))] * 4
         + [sem(nx + ny), sem(2), sem(nx + ny), sem(2), sem(nz), sem(1)]
         + [sem(nz)] * 2 + [sem(ny)] * 2 + [sem(nx)] * 2 + [sem(nz)] * 2
@@ -881,13 +836,11 @@
     rx, rb, rc, rdt, gy = resp_x[0, 0], resp_b[0, 0], resp_c[0, 0], resp_dt[0, 0], grad_out[0, 0]
     bias, alog = dt_bias[None], a_log[None]
     factor = advantages * float(nz * TOK) / lengths.astype(F32)
-    fresh, entry, end, tile = first_call(lengths, rx, rb, rc, rdt, gy, px, pb, pdt, ps, bias, alog)
     pdx, pdb, pdd, rdx, rdb, rdc, rdd, small = main_call(
-        mesh_shape, lengths, factor, fresh, entry, end, tile,
-        rx, rb, rc, rdt, gy, px, pb, pdt, ps, bias, alog, skip[None],
+        mesh_shape, lengths, factor, rx, rb, rc, rdt.T, gy, px, pb, pdt.T, ps, bias, alog, skip[None],
     )
     return (
-        pdx[None], pdb[None], pdd[None], rdx[None, None], rdb[None, None], rdc[None, None], rdd[None, None],
+        pdx[None], pdb[None], pdd.T[None], rdx[None, None], rdb[None, None], rdc[None, None], rdd.T[None, None],
         small[0, :NH], small[1, :NH], small[2, :NH],
     )
 

time: 188 us -> 160 us (0.85)
  Pallas kernels: 171 us -> 149 us
  local copies, waits for them, and re-layouts: 14.3 us -> 9.17 us
    pallas_call x1 -> x0, Pallas kernels: 15.4 us -> none  [first_call(): pl.pallas_call(first_kernel, grid=(CHUNKS,), out_shape=(shape, shape, sha...]
    pallas_call x1, Pallas kernels: 155 us -> 149 us  [main_call(): pl.pallas_call(functools.partial(main_kernel, nz, nx, ny), out_shape=(out...]
    unnamed x17 -> x19, local copies, waits for them, and re-layouts: 13 us -> 7.85 us
where the time goes in v3:
time: 160 us
  Pallas kernels  149 us (93%)
  local copies, waits for them, and re-layouts  9.17 us (6%)
  between operations  2 us (1%)
    pallas_call x1, Pallas kernels, main_call(): pl.pallas_call(functools.partial(main_kernel, nz, nx, ny), out_shape=(out...  149 us
    unnamed x19, local copies, waits for them, and re-layouts  7.85 us

profile of v3, /device:TPU:1, one launch (start us, length us, event | category | flops | bytes accessed | tf_op | source)
XLA Modules:
  0.0 160.1 jit_solution(6692851940008292468)
XLA Ops:
  2.0 149.0 %main.1 = (bf16[256,4096]{1,0:T(8,128)(2,1)}, f32[256,128]{1,0:T(8,128)}, f32[64,256]{1,0:T(8,128)}, bf16[256,4096]{1,0:T(8,128)(2,1)}, f32[256,128]{1,0:T(8,128...) custom-call(s32[1,1]{1,0:T(1,128)S(6)} %copy.31.len_ref, f32[1,1]{1,0:T(1,128)S(6)} %div.3.fac_ref, ...), custom_call_target="tpu_custom_call" | custom-call | tf_op jit(solution)/shard_map/main/pallas_call | solution.py:785
  151.0 1.3 slice_bitcast_fusion
  152.3 0.0 copy-start.3
  152.3 0.0 copy-start.5
  152.3 0.0 copy-start
  152.3 3.3 %copy.33 = bf16[1,256,4096]{2,1,0:T(8,128)(2,1)} copy(bf16[1,256,4096]{2,1,0:T(8,128)(2,1)} %bitcast.37) | data formatting | bytes 4194304
  155.6 0.0 copy-done.3
  155.6 0.7 copy.34
  156.2 0.0 copy-done.5
  156.2 0.6 copy.35
  156.9 0.0 copy-done
  156.9 0.0 copy-start.2
  156.9 0.0 copy-start.1
  156.9 0.0 copy-start.4
  156.9 1.3 copy.36
  158.2 0.0 copy-done.2
  158.2 0.7 copy.37
  158.8 0.0 copy-done.1
  158.8 0.7 copy.38
  159.5 0.0 copy-done.4
  159.5 0.6 copy.39
Async XLA Ops:
  152.3 3.3 %copy-start.3 = (f32[256,128]{1,0:T(8,128)S(1)}, f32[256,128]{1,0:T(8,128)}, u32[]{:S(2)}) copy-start(f32[256,128]{1,0:T(8,128)} %get-tuple-element.19) | copy-start | bytes 393220
  152.3 3.9 %copy-start.5 = (f32[64,256]{1,0:T(8,128)S(1)}, f32[64,256]{1,0:T(8,128)}, u32[]{:S(2)}) copy-start(f32[64,256]{1,0:T(8,128)} %get-tuple-element.20) | copy-start | bytes 196612
  152.3 4.6 %copy-start = (bf16[256,4096]{1,0:T(8,128)(2,1)S(1)}, bf16[256,4096]{1,0:T(8,128)(2,1)}, u32[]{:S(2)}) copy-start(bf16[256,4096]{1,0:T(8,128)(2,1)} %get-tuple-element.21) | copy-start | bytes 6291460
  156.9 1.3 copy-start.2
  156.9 2.0 %copy-start.1 = (f32[256,128]{1,0:T(8,128)S(1)}, f32[256,128]{1,0:T(8,128)}, u32[]{:S(2)}) copy-start(f32[256,128]{1,0:T(8,128)} %get-tuple-element.23) | copy-start | bytes 393220
  156.9 2.6 %copy-start.4 = (f32[64,256]{1,0:T(8,128)S(1)}, f32[64,256]{1,0:T(8,128)}, u32[]{:S(2)}) copy-start(f32[64,256]{1,0:T(8,128)} %get-tuple-element.24) | copy-start | bytes 196612

commit v4 on v3

--- a/solution.py
+++ b/solution.py
@@ -111,7 +111,8 @@
 
 
 LAG = 3
-MARKS = (5, 7, 8, 9, 10, 11, 12, 13)
+LATE = 5
+MARKS = (4, 5, 7, 9, 11, 13, 15)
 
 
 def main_kernel(
@@ -222,13 +223,10 @@
         pbt[...] = pb_ref[...].astype(F32).T.astype(BF16)
         pecat[...] = cat2(jnp.broadcast_to(tile_ref[1:2, :NH], (NS, NH)))
 
-        def one(c, carry):
-            spread = spreader(c, 2 * NH)
-            hi, lo = split2(nn(pwcat[...], spread) * chunk_of(px_ref, c).astype(F32))
-            put(end_in, c, nn(pecat[...], spread) * saved_state(c) + (nn(pbt[...], hi) + nn(pbt[...], lo)))
-            return carry
-
-        lax.fori_loop(0, CHUNKS, one, 0, unroll=2)
+    def add_last(c):
+        spread = spreader(c, 2 * NH)
+        hi, lo = split2(nn(pwcat[...], spread) * chunk_of(px_ref, c).astype(F32))
+        put(end_in, c, nn(pecat[...], spread) * saved_state(c) + (nn(pbt[...], hi) + nn(pbt[...], lo)))
 
     prepare()
     pl.semaphore_wait(barrier, len(partners))
@@ -372,6 +370,10 @@
         @pl.when(source)
         def _():
             last_state()
+
+    def end_1():
+        @pl.when(source)
+        def _():
             start(end1())
 
     def do2():
@@ -719,6 +721,11 @@
 
         step(2 * j)
 
+        @pl.when(source & (j < 4))
+        def _():
+            for k in range(4):
+                add_last(4 * j + k)
+
         @pl.when(j < CHUNKS)
         def _():
             alone(j)
@@ -729,23 +736,35 @@
         def _():
             with_grad(j - first_full)
 
+        return carry
+
+    def late_turn(j, carry):
+        turn(j, carry)
+        k = j - (turns - LATE)
+
+        for i in range(2):
+            with_state(2 * k + i)
+        for i in range(3):
+            prompt(3 * k + i)
         return carry
 
     done = 0
     acts = (
-        lambda: (do2(), end_2()), lambda: (do3(), end_3()), end_4, do4,
-        lambda: spread_5(1), lambda: spread_5(0), lambda: spread_6(1), lambda: spread_6(0),
+        end_1, do2, lambda: (do3(), end_2()), lambda: (do4(), end_3()), lambda: (spread_5(0), end_4()),
+        lambda: (spread_6(0), spread_5(1)), lambda: spread_6(1),
     )
     for mark, act in zip(MARKS, acts):
+        mark = min(mark, turns - LATE)
         lax.fori_loop(done, mark, turn, 0)
         act()
         done = mark
-    lax.fori_loop(done, turns, turn, 0)
+    lax.fori_loop(done, turns - LATE, turn, 0)
+    wait_recv(phase6(0))
     wait_recv(phase6(1))
-    looped(with_state, 0, CHUNKS)
+    lax.fori_loop(turns - LATE, turns, late_turn, 0)
+    looped(with_state, 2 * LATE, CHUNKS)
+    looped(prompt, 3 * LATE, CHUNKS)
     close_resp()
-    wait_recv(phase6(0))
-    looped(prompt, 0, CHUNKS)
     close_prompt()
     part = CHUNKS // 4
     pending = gather(sx, x, nx, xs_s, xs_r, [dev(z, t, y) for t in xs], lambda: looped(prompt_rest, 0, part))
@@ -781,18 +800,10 @@
     b = lambda *shape: pltpu.VMEM(shape, BF16)
     buf = lambda *lead: pltpu.VMEM(lead + (128,), F32)
     sem = lambda n: pltpu.SemaphoreType.DMA((n,))
-    out = jax.ShapeDtypeStruct
     return pl.pallas_call(
         functools.partial(main_kernel, nz, nx, ny),
         out_shape=(
-            out((TOK, NH * HD), BF16),
-            out((TOK, NS), F32),
-            out((NH, TOK), F32),
-            out((TOK, NH * HD), BF16),
-            out((TOK, NS), F32),
-            out((TOK, NS), F32),
-            out((NH, TOK), F32),
-            out((8, 128), F32),
+            b(TOK, NH * HD), v(TOK, NS), v(NH, TOK), b(TOK, NH * HD), v(TOK, NS), v(TOK, NS), v(NH, TOK), v(8, 128),
         ),
         in_specs=[smem] * 2 + [vmem] * 12,
         out_specs=(vmem,) * 8,

time: 160 us -> 149 us (0.931)
  Pallas kernels: 149 us -> 140 us
  local copies, waits for them, and re-layouts: 9.17 us -> 6.38 us
    pallas_call x1, Pallas kernels: 149 us -> 140 us  [main_call(): pl.pallas_call(functools.partial(main_kernel, nz, nx, ny), out_shape=(b(T...]
    unnamed x19 -> x7, local copies, waits for them, and re-layouts: 7.85 us -> 5.86 us
where the time goes in v4:
time: 149 us
  Pallas kernels  140 us (94%)
  local copies, waits for them, and re-layouts  6.38 us (4%)
  between operations  1.99 us (1%)
    pallas_call x1, Pallas kernels, main_call(): pl.pallas_call(functools.partial(main_kernel, nz, nx, ny), out_shape=(b(T...  140 us
    unnamed x7, local copies, waits for them, and re-layouts  5.86 us

profile of v4, /device:TPU:1, one launch (start us, length us, event | category | flops | bytes accessed | tf_op | source)
XLA Modules:
  0.0 148.5 jit_solution(15383371828578636361)
XLA Ops:
  2.0 140.1 %main.1 = (bf16[256,4096]{1,0:T(8,128)(2,1)S(1)}, f32[256,128]{1,0:T(8,128)S(1)}, f32[64,256]{1,0:T(8,128)S(1)}, bf16[256,4096]{1,0:T(8,128)(2,1)S(1)}, f32[256,...) custom-call(s32[1,1]{1,0:T(1,128)S(6)} %copy.38.len_ref, ...), custom_call_target="tpu_custom_call" | custom-call | tf_op jit(solution)/shard_map/main/pallas_call | solution.py:803
  142.1 0.5 slice_bitcast_fusion
  142.7 1.3 copy.31
  144.0 1.3 copy.34
  145.3 0.7 copy.32
  145.9 0.7 copy.35
  146.6 0.7 copy.36
  147.3 0.6 copy.33
  147.9 0.6 copy.37
